TPU v7x, 256 devices: a whole 4x4x8 slice. The times are simulated.
256 devices in a mesh: track: 16 (over y, z_hi), rep: 16 (over x, z_lo, core).
Axes of the slice: x: 4, y: 4, z: 8 (z_hi: 4, z_lo: 2; z = z_hi * 2 + z_lo), core: 2. Of those that a mesh axis runs over, the one named last changes fastest.
Arguments:
- features: bfloat16 [16, 32, 32, 2048], P('rep', None, None, 'track'), may hold values from -6 to 6
- kernel_one: bfloat16 [5, 5, 32, 128], replicated, may hold values from -0.21875 to 0.21875
- kernel_two: bfloat16 [3, 3, 128, 128], replicated, may hold values from -0.1875 to 0.1875
- cotangent: bfloat16 [16, 128, 32, 2048], P('rep', None, None, 'track'), may hold values from -0.005859375 to 0.005859375
Outputs:
- feature_map: bfloat16 [16, 128, 32, 2048], P('rep', None, None, 'track')
- grad_one: float32 [5, 5, 32, 128], replicated
- grad_two: float32 [3, 3, 128, 128], replicated
All inputs are finite; a program needn't handle non-finite values.
Results may differ from a plain program's by a relative error of at most 0.006.
Values may be sent and summed in bfloat16 or wider, within the bound.
No kernel may reach another device: no remote copies, remote signals or barrier semaphores. Data moves between devices by JAX's collectives and lax.ppermute only.
A program may use at most 64 MiB of HBM per device.

v0:
```python
import jax
import jax.numpy as jnp
from jax import lax
from jax.sharding import PartitionSpec as P

scale_a = 0.7978845608
scale_b = 0.044715


def extended(block, sides, width):
    for axis, dim in sides:
        count = lax.axis_size(axis)
        forward = [(i, i + 1) for i in range(count - 1)]
        backward = [(target, source) for source, target in forward]
        low = lax.ppermute(
            lax.slice_in_dim(block, block.shape[dim] - width, None, axis=dim), axis, forward
        )
        high = lax.ppermute(lax.slice_in_dim(block, 0, width, axis=dim), axis, backward)
        block = jnp.concatenate([low, block, high], axis=dim)
    return block


def gelu(values):
    tangent = jnp.tanh(scale_a * (values + scale_b * values * values * values))
    return 0.5 * values * (1.0 + tangent)


def gelu_slope(values):
    tangent = jnp.tanh(scale_a * (values + scale_b * values * values * values))
    return 0.5 * (1.0 + tangent) + 0.5 * values * (1.0 - tangent * tangent) * scale_a * (
        1.0 + 3.0 * scale_b * values * values
    )


def convolve(lhs, kernel, dilation):
    return lax.conv_general_dilated(
        lhs,
        kernel,
        (1, 1),
        ((2, 2), (0, 0)),
        rhs_dilation=(dilation, dilation),
        dimension_numbers=("NCHW", "HWIO", "NCHW"),
        preferred_element_type=jnp.float32,
    )


def pad_rows(array):
    return jnp.pad(array, ((0, 0), (0, 0), (2, 2), (0, 0)))


def kernel_grad(padded, delta, taps, dilation):
    row_count = delta.shape[2]
    col_count = delta.shape[3]
    row_list = []
    for row_tap in range(taps):
        col_list = []
        for col_tap in range(taps):
            window = padded[
                :,
                :,
                dilation * row_tap : dilation * row_tap + row_count,
                dilation * col_tap : dilation * col_tap + col_count,
            ]
            col_list.append(
                jnp.einsum("nchw,nfhw->cf", window, delta, preferred_element_type=jnp.float32)
            )
        row_list.append(jnp.stack(col_list))
    return jnp.stack(row_list)


def on_device(features, kernel_one, kernel_two, cotangent):
    x_cols = extended(features, (("track", 3),), 2)
    pre_one = convolve(x_cols, kernel_one, 1)
    hidden = gelu(pre_one).astype(jnp.bfloat16)
    h_cols = extended(hidden, (("track", 3),), 2)
    pre_two = convolve(h_cols, kernel_two, 2)
    feature_map = gelu(pre_two).astype(jnp.bfloat16)
    delta_two = (cotangent.astype(jnp.float32) * gelu_slope(pre_two)).astype(jnp.bfloat16)
    local_two = kernel_grad(pad_rows(h_cols), delta_two, 3, 2)
    d_cols = extended(delta_two, (("track", 3),), 2)
    flipped = jnp.transpose(kernel_two[::-1, ::-1], (0, 1, 3, 2))
    back_hidden = convolve(d_cols, flipped, 2)
    delta_one = (back_hidden * gelu_slope(pre_one)).astype(jnp.bfloat16)
    local_one = kernel_grad(pad_rows(x_cols), delta_one, 5, 1)
    grad_one, grad_two = lax.psum((local_one, local_two), ("track", "rep"))
    return (feature_map, grad_one, grad_two)


def solution(mesh):
    placed = (P("rep", None, None, "track"), P(), P(), P("rep", None, None, "track"))
    return jax.shard_map(
        on_device,
        mesh=mesh,
        in_specs=placed,
        out_specs=(P("rep", None, None, "track"), P(), P()),
        check_vma=False,
    )
```

profile of v0, /device:TPU:1, one launch (start us, length us, event | category | flops | bytes accessed | tf_op | source)
XLA Modules:
  0.0 389.4 jit_solution(2140565538895657970)
XLA Ops:
  7.2 1.9 constant_dynamic-update-slice_fusion.1
  9.3 1.3 collective-permute-start.1
  10.6 6.4 %collective-permute-start = (bf16[1,32,32,2]{3,1,2,0:T(8,128)(2,1)S(1)}, bf16[1,32,32,2]{3,1,2,0:T(8,128)(2,1)S(1)}, u32[]{:S(2)}, u32[]{:S(2)}) collective-permute-start(bf16[1,32,32,2]{3,1,2,0:T(8,128)(2,1)S(1)} %get-tuple-element.19), channel_id=1, source_target_pairs={{0,16},{16,32},{32,48},{48,64},{64,80},{80,96},{96,112},{112,128},... | collective-permute-start | bytes 12296 | tf_op jit(solution)/shard_map/ppermute | solution.py:15
  17.0 2.3 copy.69
  19.3 6.7 %collective-permute-done.1 = bf16[1,32,32,2]{3,1,2,0:T(8,128)(2,1)S(1)} collective-permute-done((bf16[1,32,32,2]{3,1,2,0:T(8,128)(2,1)S(1)}, bf16[1,32,32,2]{3,1,2,0:T(8,128)(2,1)S(1)}, u32[]{:S(2)}, u32[]{:S(2)}) %collective-permute-start.1) | collective-permute-done | bytes 4128 | tf_op jit(solution)/shard_map/ppermute | solution.py:18
  26.7 1.4 copy.92
  28.3 1.7 copy.58
  30.0 1.0 slice.177
  31.1 6.9 %multiply_convert_fusion.1 = (bf16[32,8,17,128]{3,1,2,0:T(8,128)(2,1)S(1)}, f32[32,8,17,128]{3,1,2,0:T(8,128)}) fusion(pred[8,17]{0,1:T(8,128)(4,1)S(1)} %copy-done.15, bf16[5,5,32,128]{3,2,1,0:T(8,128)(2,1)S(1)} %copy-done.14, bf16[32,32,1,7,4]{0,3,4,1,2:T(8,128)(2,1)S(1)} %slice.177, bf16[32,32,1,8,17]{0,3,4,1,2:T(8,128)(2,1)} %copy.58), kind=kOutput, calls=%fused_computation.22 | convolution fusion | flops 864468992 | bytes 3883144 | tf_op jit(solution)/shard_map/conv_general_dilated | solution.py:36
  38.2 1.0 copy.90
  39.2 1.4 fusion.196
  40.6 1.6 copy.62
  42.2 1.3 collective-permute-start.3
  43.9 7.9 %collective-permute-start.2 = (bf16[1,128,32,2]{1,2,3,0:T(8,128)(2,1)S(1)}, bf16[1,128,32,2]{1,2,3,0:T(8,128)(2,1)S(1)}, u32[]{:S(2)}, u32[]{:S(2)}) collective-permute-start(bf16[1,128,32,2]{1,2,3,0:T(8,128)(2,1)S(1)} %copy.61), channel_id=1, source_target_pairs={{0,16},{16,32},{32,48},{48,64},{64,80},{80,96},{96,112},{112,128},... | collective-permute-start | bytes 49160 | tf_op jit(solution)/shard_map/ppermute | solution.py:15
  51.9 1.7 constant_dynamic-update-slice_fusion
  54.1 1.4 copy.63
  55.5 3.9 fusion.230
  59.4 2.5 pad_maximum_fusion
  61.9 3.0 copy.93
  65.6 5.0 %fusion.12 = (f32[32,8,17,128]{3,1,2,0:T(8,128)S(1)}, bf16[32,8,17,128]{3,1,2,0:T(8,128)(2,1)}) fusion(pred[8,17]{0,1:T(8,128)(4,1)S(1)} %copy-done.15, bf16[3,3,128,128]{3,2,1,0:T(8,128)(2,1)S(1)} %copy-done, bf16[128,32,1,7,4]{0,3,4,1,2:T(8,128)(2,1)S(1)} %slice.181, bf16[128,32,1,8,17]{0,3,4,1,2:T(8,128)(2,1)S(1)} %copy.67), kind=kOutput, calls=%fused_computation.18 | convolution fusion | flops 1245249536 | bytes 4980872 | tf_op jit(solution)/shard_map/conv_general_dilated | solution.py:36
  73.2 1.9 copy.78
  75.2 2.3 convolution_bitcast_fusion
  82.8 1.3 collective-permute-start.5
  84.1 7.1 %collective-permute-start.4 = (bf16[1,128,32,2]{1,2,3,0:T(8,128)(2,1)S(1)}, bf16[1,128,32,2]{1,2,3,0:T(8,128)(2,1)S(1)}, u32[]{:S(2)}, u32[]{:S(2)}) collective-permute-start(bf16[1,128,32,2]{1,2,3,0:T(8,128)(2,1)S(1)} %get-tuple-element.13), channel_id=1, source_target_pairs={{0,16},{16,32},{32,48},{48,64},{64,80},{80,96},{96,112},{112,128},... | collective-permute-start | bytes 49160 | tf_op jit(solution)/shard_map/ppermute | solution.py:15
  91.2 0.9 pad_maximum_fusion.3
  93.0 0.9 copy-done.17
  93.9 3.9 %fusion.7 = bf16[32,8,17,128]{3,1,2,0:T(8,128)(2,1)S(1)} fusion(f32[32,8,17,128]{3,1,2,0:T(8,128)S(1)} %copy-done.17, bf16[3,3,128,128]{3,2,1,0:T(8,128)(2,1)S(1)} %copy-done, bf16[128,32,1,7,4]{0,3,4,1,2:T(8,128)(2,1)S(1)} %slice.186, bf16[128,32,1,8,17]{0,3,4,1,2:T(8,128)(2,1)S(1)} %copy.72, pred[8,17]{0,1:T(8,128)(4,1)S(1)} %copy-done.16), kind=kOutput, calls=%fused_computation.13 | convolution fusion | flops 1245806592 | bytes 4980872 | tf_op jit(solution)/shard_map/conv_general_dilated | solution.py:36
  98.1 1.0 copy.91
  114.7 2.3 copy.89
  117.0 261.9 %all-reduce.5.cloned.1.call-done = (f32[5,5,32,128]{3,2,1,0:T(8,128)}, f32[3,3,128,128]{3,2,1,0:T(8,128)}) async-done(((f32[5,5,32,128]{3,2,1,0:T(8,128)}, f32[3,3,128,128]{3,2,1,0:T(8,128)}), (f32[5,5,32,128]{3,2,1,0:T(8,128)}, f32[3,3,128,128]{3,2,1,0:T(8,128)})) %all-reduce.5.cloned.1.call-update) | async-done | bytes 999440 | tf_op jit(solution)/shard_map/psum | solution.py:85
  378.9 1.8 copy.125
  380.7 1.9 copy.126
  (103 shorter events, 27.4 us)
Async XLA Ops:
  7.2 58.5 %copy-start = (bf16[3,3,128,128]{3,2,1,0:T(8,128)(2,1)S(1)}, bf16[3,3,128,128]{3,2,1,0:T(8,128)(2,1)}, u32[]{:S(2)}) copy-start(bf16[3,3,128,128]{3,2,1,0:T(8,128)(2,1)} %param.6) | copy-start | bytes 884740
  7.2 9.8 %copy-start.12 = (bf16[1,128,32,128]{3,2,1,0:T(8,128)(2,1)S(1)}, bf16[1,128,32,128]{3,2,1,0:T(8,128)(2,1)}, u32[]{:S(2)}) copy-start(bf16[1,128,32,128]{3,2,1,0:T(8,128)(2,1)} %param.7) | copy-start | bytes 3145732
  7.2 371.7 %all-reduce.5.cloned.1.call-start = ((), (), s32[]{:S(2)}) async-start(), calls=%async_computation | async-start | bytes 1998848 | tf_op jit(solution)/shard_map/psum | solution.py:85
  9.3 16.7 %collective-permute-start.1 = (bf16[1,32,32,2]{3,1,2,0:T(8,128)(2,1)S(1)}, bf16[1,32,32,2]{3,1,2,0:T(8,128)(2,1)S(1)}, u32[]{:S(2)}, u32[]{:S(2)}) collective-permute-start(bf16[1,32,32,2]{3,1,2,0:T(8,128)(2,1)S(1)} %get-tuple-element.20), channel_id=1, source_target_pairs={{16,0},{32,16},{48,32},{64,48},{80,64},{96,80},{112,96},{128,112},... | collective-permute-start | bytes 12296 | tf_op jit(solution)/shard_map/ppermute | solution.py:18
  10.6 15.4 %collective-permute-start = (bf16[1,32,32,2]{3,1,2,0:T(8,128)(2,1)S(1)}, bf16[1,32,32,2]{3,1,2,0:T(8,128)(2,1)S(1)}, u32[]{:S(2)}, u32[]{:S(2)}) collective-permute-start(bf16[1,32,32,2]{3,1,2,0:T(8,128)(2,1)S(1)} %get-tuple-element.19), channel_id=1, source_target_pairs={{0,16},{16,32},{32,48},{48,64},{64,80},{80,96},{96,112},{112,128},... | collective-permute-start | bytes 12296 | tf_op jit(solution)/shard_map/ppermute | solution.py:15
  26.0 0.7 copy-start.11
  28.0 3.0 copy-start.15
  28.3 2.8 copy-start.14
  42.2 11.4 %collective-permute-start.3 = (bf16[1,128,32,2]{1,2,3,0:T(8,128)(2,1)S(1)}, bf16[1,128,32,2]{1,2,3,0:T(8,128)(2,1)S(1)}, u32[]{:S(2)}, u32[]{:S(2)}) collective-permute-start(bf16[1,128,32,2]{1,2,3,0:T(8,128)(2,1)S(1)} %copy.62), channel_id=1, source_target_pairs={{16,0},{32,16},{48,32},{64,48},{80,64},{96,80},{112,96},{128,112},... | collective-permute-start | bytes 49160 | tf_op jit(solution)/shard_map/ppermute | solution.py:18
  43.9 10.2 %collective-permute-start.2 = (bf16[1,128,32,2]{1,2,3,0:T(8,128)(2,1)S(1)}, bf16[1,128,32,2]{1,2,3,0:T(8,128)(2,1)S(1)}, u32[]{:S(2)}, u32[]{:S(2)}) collective-permute-start(bf16[1,128,32,2]{1,2,3,0:T(8,128)(2,1)S(1)} %copy.61), channel_id=1, source_target_pairs={{0,16},{16,32},{32,48},{48,64},{64,80},{80,96},{96,112},{112,128},... | collective-permute-start | bytes 49160 | tf_op jit(solution)/shard_map/ppermute | solution.py:15
  54.1 5.3 %copy-start.2 = (bf16[1,128,32,2]{3,1,2,0:T(8,128)(2,1)}, bf16[1,128,32,2]{3,1,2,0:T(8,128)(2,1)S(1)}, u32[]{:S(2)}) copy-start(bf16[1,128,32,2]{3,1,2,0:T(8,128)(2,1)S(1)} %copy.64) | copy-start | bytes 49156
  55.5 3.9 copy-start.4
  70.7 1.2 copy-start.8
  72.2 1.0 copy-start.6
  75.2 2.3 copy-start.1
  79.7 1.2 copy-start.3
  80.9 1.3 copy-start.5
  82.1 10.0 %copy-start.7 = (bf16[1,128,32,128]{1,2,3,0:T(8,128)(2,1)S(1)}, bf16[1,128,32,128]{1,2,3,0:T(8,128)(2,1)}, u32[]{:S(2)}) copy-start(bf16[1,128,32,128]{1,2,3,0:T(8,128)(2,1)} %copy-done.6) | copy-start | bytes 3145732
  82.8 9.3 %collective-permute-start.5 = (bf16[1,128,32,2]{1,2,3,0:T(8,128)(2,1)}, bf16[1,128,32,2]{1,2,3,0:T(8,128)(2,1)S(1)}, u32[]{:S(2)}, u32[]{:S(2)}) collective-permute-start(bf16[1,128,32,2]{1,2,3,0:T(8,128)(2,1)} %get-tuple-element.14), channel_id=1, source_target_pairs={{16,0},{32,16},{48,32},{64,48},{80,64},{96,80},{112,96},{128,112},... | collective-permute-start | bytes 49160 | tf_op jit(solution)/shard_map/ppermute | solution.py:18
  84.1 8.0 %collective-permute-start.4 = (bf16[1,128,32,2]{1,2,3,0:T(8,128)(2,1)S(1)}, bf16[1,128,32,2]{1,2,3,0:T(8,128)(2,1)S(1)}, u32[]{:S(2)}, u32[]{:S(2)}) collective-permute-start(bf16[1,128,32,2]{1,2,3,0:T(8,128)(2,1)S(1)} %get-tuple-element.13), channel_id=1, source_target_pairs={{0,16},{16,32},{32,48},{48,64},{64,80},{80,96},{96,112},{112,128},... | collective-permute-start | bytes 49160 | tf_op jit(solution)/shard_map/ppermute | solution.py:15
  92.3 0.7 copy-start.16
  92.3 1.6 copy-start.17
  104.9 1.5 copy-start.13
  105.4 1.5 copy-start.9
  110.8 3.6 copy-start.10
Sparse Core Ops, SparseCore 0:
  114.6 264.2 all-reduce.4
where the time goes:
time: 391 us; the launch traced here: 389 us
  waiting for transfers between devices  269 us (69%)
  local copies, waits for them, and re-layouts  38.4 us (10%)
  matrix products  34.4 us (9%)
  starting transfers between devices  25.3 us (6%)
  between operations  14.7 us (4%)
  other arithmetic  8.07 us (2%)
    psum x1, waiting for transfers between devices, on_device(): grad_one, grad_two = lax.psum((local_one, local_two), ('track', 'rep'))  262 us
    unnamed x49, local copies, waits for them, and re-layouts  22.4 us
    ppermute x3, starting transfers between devices, extended(): lax.ppermute(lax.slice_in_dim(block, block.shape[dim] - width, None, axis...  21.4 us
    dot_general x34, matrix products, kernel_grad(): jnp.einsum('nchw,nfhw->cf', window, delta, preferred_element_type=jnp.flo...  18.6 us
    conv_general_dilated x3, matrix products, convolve(): lax.conv_general_dilated(lhs, kernel, (1, 1), ((2, 2), (0, 0)), rhs_dilat...  15.8 us
  transfers between devices with their start and end apart: 7, of which 2 were waited for; matrix products, arithmetic and copies ran while one was open for 2% of the time, Pallas kernels for 0%

commit v1 on v0

v1 whole, which is shorter than its diff:
```python
import jax
import jax.numpy as jnp
from jax import lax
from jax.experimental import pallas as pl
from jax.experimental.pallas import tpu as pltpu
from jax.sharding import Mesh, PartitionSpec as P

scale_a = 0.7978845608
scale_b = 0.044715
BF = jnp.bfloat16
F32 = jnp.float32
ONE = 12
TWO = 8
BACK = 12
SUM_TWO = 16
SUM_ONE = 12


def gelu_and_slope(v):
    v2 = v * v
    t = jnp.tanh(v * (scale_a + (scale_a * scale_b) * v2))
    half = 0.5 * v
    value = half + half * t
    slope = 0.5 + 0.5 * t + half * (1.0 - t * t) * (scale_a + (3.0 * scale_a * scale_b) * v2)
    return value, slope


def shifted(v, shift):
    rows = v.shape[1]
    h = lax.broadcasted_iota(jnp.int32, v.shape, 1)
    rolled = pltpu.roll(v, (-shift) % rows, 1)
    keep = (h < rows - shift) if shift > 0 else (h >= -shift)
    return jnp.where(keep, rolled, 0.0)


def flat(v):
    return v.reshape(v.shape[0] * v.shape[1], v.shape[2])


def over_rows(a, b):
    return lax.dot_general(a, b, (((0,), (0,)), ((), ())), preferred_element_type=F32)


def block_kernel(
    place, low, middle, high, k1, k2, k2t, cot, fmap, keep, send,
    xe, taps, bottom, tail, hid, slope, delta, dlast, acc2, acc1, total,
):
    xe[0:4] = low[...]
    xe[4:132] = middle[...]
    xe[132:136] = high[...]

    def row_taps(n, carry):
        at = pl.ds(n * 8, 8)
        v = xe[at].astype(F32)
        lane = lax.broadcasted_iota(jnp.int32, v.shape, 2)
        taps[at] = jnp.where(
            lane < 64,
            jnp.where(lane < 32, shifted(v, -2), shifted(v, -1)),
            jnp.where(lane < 96, v, shifted(v, 1)),
        ).astype(BF)
        bottom[at] = shifted(v, 2).astype(BF)
        return carry

    lax.fori_loop(0, 17, row_taps, 0)

    def last_row_taps(n, carry):
        at = n * 12
        lane = lax.broadcasted_iota(jnp.int32, (12, 32, 128), 2)
        s = [bottom[pl.ds(at + j, 12)] for j in range(4)]
        tail[pl.ds(at, 12)] = jnp.where(
            lane < 64, jnp.where(lane < 32, s[0], s[1]), jnp.where(lane < 96, s[2], s[3])
        )
        return carry

    lax.fori_loop(0, 11, last_row_taps, 0)

    def windows_one(at, n):
        parts = [taps[pl.ds(at + j, n)] for j in range(5)]
        parts += [tail[pl.ds(at, n)], bottom[pl.ds(at + 4, n)]]
        return jnp.concatenate([flat(x) for x in parts], axis=1)

    def windows_two(at, n):
        parts = [hid[i, pl.ds(at + 2 * j, n)] for i in range(3) for j in range(3)]
        return jnp.concatenate([flat(x) for x in parts], axis=1)

    def first(n, carry):
        at = n * ONE
        pre = jnp.dot(windows_one(at, ONE), k1[...], preferred_element_type=F32)
        h, s = gelu_and_slope(pre.reshape(ONE, 32, 128))
        slope[pl.ds(at, ONE)] = s
        hid[0, pl.ds(at, ONE)] = shifted(h, -2).astype(BF)
        hid[1, pl.ds(at, ONE)] = h.astype(BF)
        hid[2, pl.ds(at, ONE)] = shifted(h, 2).astype(BF)
        return carry

    lax.fori_loop(0, 132 // ONE, first, 0)

    @pl.when(place[0] == 0)
    def _():
        hid[:, 0:2] = jnp.zeros((3, 2, 32, 128), BF)
        slope[0:2] = jnp.zeros((2, 32, 128), F32)

    @pl.when(place[1] == 0)
    def _():
        hid[:, 130:132] = jnp.zeros((3, 2, 32, 128), BF)
        slope[130:132] = jnp.zeros((2, 32, 128), F32)

    delta[:, 0:4] = jnp.zeros((3, 4, 32, 128), BF)
    delta[:, 132:136] = jnp.zeros((3, 4, 32, 128), BF)

    def second(n, carry):
        at = n * TWO
        pre = jnp.dot(windows_two(at, TWO), k2[...], preferred_element_type=F32)
        f, s = gelu_and_slope(pre.reshape(TWO, 32, 128))
        fmap[pl.ds(at, TWO)] = f.astype(BF)
        d = cot[pl.ds(at, TWO)].astype(F32) * s
        delta[0, pl.ds(at + 4, TWO)] = shifted(d, 2).astype(BF)
        delta[1, pl.ds(at + 4, TWO)] = d.astype(BF)
        delta[2, pl.ds(at + 4, TWO)] = shifted(d, -2).astype(BF)
        return carry

    lax.fori_loop(0, 128 // TWO, second, 0)

    acc2[...] = jnp.zeros(acc2.shape, F32)
    acc1[...] = jnp.zeros(acc1.shape, F32)

    def sum_two(n, carry):
        at = n * SUM_TWO
        d = flat(delta[1, pl.ds(at + 4, SUM_TWO)])
        acc2[...] += over_rows(d, windows_two(at, SUM_TWO))
        return carry

    lax.fori_loop(0, 128 // SUM_TWO, sum_two, 0)

    def back(n, carry):
        at = n * BACK
        parts = [delta[i, pl.ds(at + 4 - 2 * j, BACK)] for i in range(3) for j in range(3)]
        lhs = jnp.concatenate([flat(x) for x in parts], axis=1)
        b = jnp.dot(lhs, k2t[...], preferred_element_type=F32)
        dlast[pl.ds(at, BACK)] = (b.reshape(BACK, 32, 128) * slope[pl.ds(at, BACK)]).astype(BF)
        return carry

    lax.fori_loop(0, 132 // BACK, back, 0)

    def sum_one(n, carry):
        at = n * SUM_ONE
        d = flat(dlast[pl.ds(at, SUM_ONE)])
        acc1[...] += over_rows(d, windows_one(at, SUM_ONE))
        return carry

    lax.fori_loop(0, 132 // SUM_ONE, sum_one, 0)

    total[0:1152] = acc2[...].T
    a1 = acc1[...].T
    for i in range(5):
        for j in range(5):
            row = j * 128 + i * 32 if i < 4 else 640 + j * 32
            to = 1152 + (i * 5 + j) * 32
            total[to : to + 32] = a1[row : row + 32]
    total[1952:2048] = jnp.zeros((96, 128), F32)
    mine = pl.multiple_of(place[2] * 1024, 1024)
    other = pl.multiple_of((1 - place[2]) * 1024, 1024)
    keep[...] = total[pl.ds(mine, 1024)]
    send[...] = total[pl.ds(other, 1024)].astype(BF)


def block(place, low, middle, high, k1, k2, k2t, cot):
    vmem = pl.BlockSpec(memory_space=pltpu.VMEM)
    return pl.pallas_call(
        block_kernel,
        out_shape=(
            jax.ShapeDtypeStruct((128, 32, 128), BF),
            jax.ShapeDtypeStruct((1024, 128), F32),
            jax.ShapeDtypeStruct((1024, 128), BF),
        ),
        in_specs=[pl.BlockSpec(memory_space=pltpu.SMEM)] + [vmem] * 7,
        out_specs=(vmem, vmem, vmem),
        scratch_shapes=[
            pltpu.VMEM((136, 32, 128), BF),
            pltpu.VMEM((136, 32, 128), BF),
            pltpu.VMEM((136, 32, 128), BF),
            pltpu.VMEM((132, 32, 128), BF),
            pltpu.VMEM((3, 132, 32, 128), BF),
            pltpu.VMEM((132, 32, 128), F32),
            pltpu.VMEM((3, 136, 32, 128), BF),
            pltpu.VMEM((132, 32, 128), BF),
            pltpu.VMEM((128, 1152), F32),
            pltpu.VMEM((128, 896), F32),
            pltpu.VMEM((2048, 128), F32),
        ],
        compiler_params=pltpu.CompilerParams(vmem_limit_bytes=50 * 1024 * 1024),
        cost_estimate=pl.CostEstimate(
            flops=5_500_000_000, bytes_accessed=5_000_000, transcendentals=1_100_000
        ),
    )(place, low, middle, high, k1, k2, k2t, cot)


def kernel_rows(kernel_one, kernel_two):
    first = kernel_one[:4].transpose(1, 0, 2, 3).reshape(640, 128)
    last = kernel_one[4].reshape(160, 128)
    k1 = jnp.concatenate([first, last, jnp.zeros((96, 128), BF)], 0)
    k2 = kernel_two.reshape(1152, 128)
    k2t = kernel_two.transpose(0, 1, 3, 2).reshape(1152, 128)
    return k1, k2, k2t


def columns_first(block_of):
    return jnp.transpose(block_of[0], (2, 1, 0))


def fourfold(v):
    return jnp.tile(v, (1, 1, 4))


TRACK = ("y", "zh")
REP = ("x", "zl", "core")
CHIPS = ("y", "zh", "x", "zl")


def on_device(features, kernel_one, kernel_two, cotangent):
    at = lax.axis_index(TRACK)
    core = lax.axis_index("core")
    up = [(i, i + 1) for i in range(15)]
    down = [(i + 1, i) for i in range(15)]
    low = lax.ppermute(fourfold(columns_first(features[..., 124:])), TRACK, up)
    high = lax.ppermute(fourfold(columns_first(features[..., :4])), TRACK, down)
    middle = fourfold(columns_first(features))
    k1, k2, k2t = kernel_rows(kernel_one, kernel_two)
    place = jnp.stack([(at > 0).astype(jnp.int32), (at < 15).astype(jnp.int32), core])
    fmap, keep, send = block(place, low, middle, high, k1, k2, k2t, columns_first(cotangent))
    feature_map = jnp.transpose(fmap, (2, 1, 0))[None]
    swap = [(0, 1), (1, 0)]
    chip_sum = (keep + lax.ppermute(send, "core", swap).astype(F32)).astype(BF)
    parts = lax.all_to_all(chip_sum.reshape(128, 8, 128), CHIPS, 0, 0, tiled=True)
    mine = jnp.sum(parts.astype(F32), axis=0).astype(BF)
    spread = jnp.broadcast_to(mine[None], (128, 8, 128))
    half = lax.all_to_all(spread, CHIPS, 0, 0, tiled=True).reshape(1024, 128)
    rest = lax.ppermute(half, "core", swap)
    rows = jnp.concatenate(
        [jnp.where(core == 0, half, rest), jnp.where(core == 0, rest, half)], axis=0
    ).astype(F32)
    grad_two = rows[:1152].reshape(3, 3, 128, 128)
    grad_one = rows[1152:1952].reshape(5, 5, 32, 128)
    return (feature_map, grad_one, grad_two)


def solution(mesh):
    fine = Mesh(mesh.devices.reshape(4, 4, 4, 2, 2), TRACK + REP)
    placed = (P(REP, None, None, TRACK), P(), P(), P(REP, None, None, TRACK))
    return jax.shard_map(
        on_device,
        mesh=fine,
        in_specs=placed,
        out_specs=(P(REP, None, None, TRACK), P(), P()),
        check_vma=False,
    )
```

time: 391 us -> 101 us (0.26)
  waiting for transfers between devices: 269 us -> 1.17 us
  blocking collectives: 0 us -> 48.7 us
  matrix products: 34.4 us -> 0 us
  local copies, waits for them, and re-layouts: 38.4 us -> 10.7 us
  Pallas kernels: 0 us -> 25.7 us
  between operations: 14.7 us -> 0.81 us
  starting transfers between devices: 25.3 us -> 11.9 us
  other arithmetic: 8.07 us -> 2.13 us
    psum x1 -> x0, waiting for transfers between devices: 262 us -> none  [on_device(): grad_one, grad_two = lax.psum((local_one, local_two), ('track', 'rep'))]
    all_to_all x0 -> x2, blocking collectives: none -> 48.7 us  [the longest x1 30.2 us: on_device(): lax.all_to_all(chip_sum.reshape(128, 8, 128), CHIPS, 0, 0, tiled=True)]
    pallas_call x0 -> x1, Pallas kernels: none -> 25.7 us  [block(): pl.pallas_call(block_kernel, out_shape=(jax.ShapeDtypeStruct((128, 32, 12...]
    dot_general x34 -> x0, matrix products: 18.6 us -> none  [kernel_grad(): jnp.einsum('nchw,nfhw->cf', window, delta, preferred_element_type=jnp.flo...]
    unnamed x49 -> x8, local copies, waits for them, and re-layouts: 22.4 us -> 6.21 us
    conv_general_dilated x3 -> x0, matrix products: 15.8 us -> none  [convolve(): lax.conv_general_dilated(lhs, kernel, (1, 1), ((2, 2), (0, 0)), rhs_dilat...]
    ppermute x6 -> x4, starting transfers between devices: 25.2 us -> 11.9 us  [the longest x1 5.73 us: on_device(): low = lax.ppermute(fourfold(columns_first(features[..., 124:])), TRACK, up)]
    concatenate x4 -> x1, other arithmetic: 6.84 us -> 0.18 us  [kernel_rows(): k1 = jnp.concatenate([first, last, jnp.zeros((96, 128), BF)], 0)]
  transfers between devices with their start and end apart: 7 -> 4, of which waited for: 2 -> 1; matrix products, arithmetic and copies ran while one was open for 2% -> 8% of each run, Pallas kernels for 0% -> 0%
where the time goes in v1:
time: 101 us
  blocking collectives  48.7 us (48%)
  Pallas kernels  25.7 us (25%)
  starting transfers between devices  11.9 us (12%)
  local copies, waits for them, and re-layouts  10.7 us (11%)
  other arithmetic  2.13 us (2%)
  waiting for transfers between devices  1.17 us (1%)
    all_to_all x1, blocking collectives, on_device(): lax.all_to_all(chip_sum.reshape(128, 8, 128), CHIPS, 0, 0, tiled=True)  30.2 us
    pallas_call x1, Pallas kernels, block(): pl.pallas_call(block_kernel, out_shape=(jax.ShapeDtypeStruct((128, 32, 12...  25.7 us
    all_to_all x1, blocking collectives, on_device(): half = lax.all_to_all(spread, CHIPS, 0, 0, tiled=True).reshape(1024, 128)  18.4 us
    unnamed x8, local copies, waits for them, and re-layouts  6.21 us
    ppermute x1, starting transfers between devices, on_device(): low = lax.ppermute(fourfold(columns_first(features[..., 124:])), TRACK, up)  5.73 us
    ppermute x1, starting transfers between devices, on_device(): rest = lax.ppermute(half, 'core', swap)  3.41 us
    transpose x4, local copies, waits for them, and re-layouts, columns_first(): return jnp.transpose(block_of[0], (2, 1, 0))  2.07 us
  transfers between devices with their start and end apart: 4, of which 1 were waited for; matrix products, arithmetic and copies ran while one was open for 8% of the time, Pallas kernels for 0%

profile of v1, /device:TPU:1, one launch (start us, length us, event | category | flops | bytes accessed | tf_op | source)
XLA Modules:
  0.0 101.1 jit_solution(15452526925411360997)
XLA Ops:
  0.6 1.2 %slice_bitcast_fusion = (bf16[4,32,32]{0,1,2:T(8,128)(2,1)S(1)}, bf16[4,32,32]{0,1,2:T(8,128)(2,1)S(1)}) fusion(bf16[1,32,32,128]{3,2,1,0:T(8,128)(2,1)} %param.4), kind=kLoop, calls=%fused_computation.4 | loop fusion | bytes 32768 | tf_op jit(solution)/shard_map/transpose | solution.py:208
  1.8 0.4 copy.14
  2.2 0.1 tile.13
  2.4 5.7 %collective-permute-start = (bf16[4,32,128]{2,1,0:T(8,128)(2,1)S(1)}, bf16[4,32,128]{2,1,0:T(8,128)(2,1)S(1)}, u32[]{:S(2)}, u32[]{:S(2)}) collective-permute-start(bf16[4,32,128]{2,1,0:T(8,128)(2,1)S(1)} %tile.13), channel_id=1, source_target_pairs={{0,16},{16,32},{32,48},{48,64},{64,80},{80,96},{96,112},{112,128},... | collective-permute-start | bytes 98312 | tf_op jit(solution)/shard_map/ppermute | solution.py:225
  8.1 0.4 copy.16
  8.6 0.1 tile.32
  8.7 1.3 %collective-permute-start.1 = (bf16[4,32,128]{2,1,0:T(8,128)(2,1)S(1)}, bf16[4,32,128]{2,1,0:T(8,128)(2,1)S(1)}, u32[]{:S(2)}, u32[]{:S(2)}) collective-permute-start(bf16[4,32,128]{2,1,0:T(8,128)(2,1)S(1)} %tile.32), channel_id=1, source_target_pairs={{16,0},{32,16},{48,32},{64,48},{80,64},{96,80},{112,96},{128,112},... | collective-permute-start | bytes 98312 | tf_op jit(solution)/shard_map/ppermute | solution.py:226
  10.0 0.0 slice-start
  10.1 0.0 copy-start.1
  10.1 0.1 pad.4.clone
  10.2 0.6 slice-done
  10.8 0.2 maximum_maximum_fusion.k1
  11.0 0.0 copy-start
  11.0 0.1 pad_add_fusion.place
  11.1 0.1 copy.15
  11.2 0.8 copy-done
  12.0 0.2 copy.18
  12.2 0.2 tile.14
  12.4 1.0 copy.20.middle
  13.3 3.2 %copy.19 = bf16[1,128,32,128]{1,2,3,0:T(8,128)(2,1)} copy(bf16[1,128,32,128]{3,2,1,0:T(8,128)(2,1)} %param.7) | data formatting | bytes 2097152 | tf_op args[3]
  16.5 0.0 collective-permute-done.low
  16.5 25.7 %shard_map.67 = (bf16[128,32,128]{2,1,0:T(8,128)(2,1)S(1)}, f32[1024,128]{1,0:T(8,128)S(1)}, bf16[1024,128]{1,0:T(8,128)(2,1)S(1)}) custom-call(s32[3]{0:T(128)S(1)} %pad_add_fusion.place, bf16[4,32,128]{2,1,0:T(8,128)(2,1)S(1)} %collective-permute-done.low, bf16[128,32,128]{2,1,0:T(8,128)(2,1)S(1)} %copy.20.middle, ...), custom_call_target="tpu_custom_call" | custom-call | flops 5500000256 | bytes 5000000 | tf_op jit(solution)/shard_map/pallas_call | solution.py:169
  42.2 1.5 %collective-permute-start.2 = (bf16[1024,128]{1,0:T(8,128)(2,1)S(1)}, bf16[1024,128]{1,0:T(8,128)(2,1)S(1)}, u32[]{:S(2)}, u32[]{:S(2)}) collective-permute-start(bf16[1024,128]{1,0:T(8,128)(2,1)S(1)} %get-tuple-element.8), channel_id=1, source_target_pairs={{0,1},{1,0},{2,3},{3,2},{4,5},{5,4},{6,7},{7,6},{8,9},{9,8},{10,11... | collective-permute-start | bytes 786440 | tf_op jit(solution)/shard_map/ppermute | solution.py:233
  43.7 1.2 %collective-permute-done.2 = bf16[1024,128]{1,0:T(8,128)(2,1)S(1)} collective-permute-done((bf16[1024,128]{1,0:T(8,128)(2,1)S(1)}, bf16[1024,128]{1,0:T(8,128)(2,1)S(1)}, u32[]{:S(2)}, u32[]{:S(2)}) %collective-permute-start.2) | collective-permute-done | bytes 262176 | tf_op jit(solution)/shard_map/ppermute | solution.py:233
  44.8 0.1 fusion.1
  44.9 30.2 %all_to_all.10 = bf16[128,8,128]{2,1,0:T(8,128)(2,1)S(1)} all-to-all(bf16[128,8,128]{2,1,0:T(8,128)(2,1)S(1)} %fusion.1), channel_id=1, replica_groups=mesh['y'=4,'zh'=4,'x'=4,'zl'=2,'core'=2] {'y','zh','x','zl'}, dimensions={0} | all-to-all | bytes 524288 | tf_op jit(solution)/shard_map/all_to_all | solution.py:234
  75.1 0.1 reduce_sum.12
  75.3 18.4 %all_to_all.11 = bf16[128,8,128]{2,1,0:T(8,128)(2,1)S(1)} all-to-all(bf16[128,8,128]{2,1,0:T(8,128)(2,1)S(1)} %broadcast_in_dim.14), channel_id=1, replica_groups=mesh['y'=4,'zh'=4,'x'=4,'zl'=2,'core'=2] {'y','zh','x','zl'}, dimensions={0} | all-to-all | bytes 524288 | tf_op jit(solution)/shard_map/all_to_all | solution.py:237
  93.7 3.4 %collective-permute-start.3 = (bf16[1024,128]{1,0:T(8,128)(2,1)S(1)}, bf16[1024,128]{1,0:T(8,128)(2,1)S(1)}, u32[]{:S(2)}, u32[]{:S(2)}) collective-permute-start(bf16[1024,128]{1,0:T(8,128)(2,1)S(1)} %bitcast.42), channel_id=1, source_target_pairs={{0,1},{1,0},{2,3},{3,2},{4,5},{5,4},{6,7},{7,6},{8,9},{9,8},{10,11... | collective-permute-start | bytes 786440 | tf_op jit(solution)/shard_map/ppermute | solution.py:238
  97.1 2.2 %copy.21 = bf16[1,128,32,128]{3,2,1,0:T(8,128)(2,1)} copy(bf16[1,128,32,128]{1,2,3,0:T(8,128)(2,1)S(1)} %bitcast.35) | data formatting | bytes 2097152
  99.4 0.8 maximum_convert_fusion
  100.2 0.9 fusion
  (12 shorter events, 0.2 us)
Async XLA Ops:
  2.4 14.2 %collective-permute-start = (bf16[4,32,128]{2,1,0:T(8,128)(2,1)S(1)}, bf16[4,32,128]{2,1,0:T(8,128)(2,1)S(1)}, u32[]{:S(2)}, u32[]{:S(2)}) collective-permute-start(bf16[4,32,128]{2,1,0:T(8,128)(2,1)S(1)} %tile.13), channel_id=1, source_target_pairs={{0,16},{16,32},{32,48},{48,64},{64,80},{80,96},{96,112},{112,128},... | collective-permute-start | bytes 98312 | tf_op jit(solution)/shard_map/ppermute | solution.py:225
  8.5 1.5 %copy-start.2 = (bf16[5,5,32,128]{3,2,1,0:T(8,128)(2,1)S(1)}, bf16[5,5,32,128]{3,2,1,0:T(8,128)(2,1)}, u32[]{:S(2)}) copy-start(bf16[5,5,32,128]{3,2,1,0:T(8,128)(2,1)} %param.5) | copy-start | bytes 614404
  8.7 7.8 %collective-permute-start.1 = (bf16[4,32,128]{2,1,0:T(8,128)(2,1)S(1)}, bf16[4,32,128]{2,1,0:T(8,128)(2,1)S(1)}, u32[]{:S(2)}, u32[]{:S(2)}) collective-permute-start(bf16[4,32,128]{2,1,0:T(8,128)(2,1)S(1)} %tile.32), channel_id=1, source_target_pairs={{16,0},{32,16},{48,32},{64,48},{80,64},{96,80},{112,96},{128,112},... | collective-permute-start | bytes 98312 | tf_op jit(solution)/shard_map/ppermute | solution.py:226
  10.0 0.8 slice-start
  10.1 1.0 %copy-start.1 = (bf16[1,32,32,128]{3,2,1,0:T(8,128)(2,1)S(1)}, bf16[1,32,32,128]{3,2,1,0:T(8,128)(2,1)}, u32[]{:S(2)}) copy-start(bf16[1,32,32,128]{3,2,1,0:T(8,128)(2,1)} %param.4) | copy-start | bytes 786436
  11.0 1.0 copy-start
  42.2 2.6 %collective-permute-start.2 = (bf16[1024,128]{1,0:T(8,128)(2,1)S(1)}, bf16[1024,128]{1,0:T(8,128)(2,1)S(1)}, u32[]{:S(2)}, u32[]{:S(2)}) collective-permute-start(bf16[1024,128]{1,0:T(8,128)(2,1)S(1)} %get-tuple-element.8), channel_id=1, source_target_pairs={{0,1},{1,0},{2,3},{3,2},{4,5},{5,4},{6,7},{7,6},{8,9},{9,8},{10,11... | collective-permute-start | bytes 786440 | tf_op jit(solution)/shard_map/ppermute | solution.py:233
  93.7 5.7 %collective-permute-start.3 = (bf16[1024,128]{1,0:T(8,128)(2,1)S(1)}, bf16[1024,128]{1,0:T(8,128)(2,1)S(1)}, u32[]{:S(2)}, u32[]{:S(2)}) collective-permute-start(bf16[1024,128]{1,0:T(8,128)(2,1)S(1)} %bitcast.42), channel_id=1, source_target_pairs={{0,1},{1,0},{2,3},{3,2},{4,5},{5,4},{6,7},{7,6},{8,9},{9,8},{10,11... | collective-permute-start | bytes 786440 | tf_op jit(solution)/shard_map/ppermute | solution.py:238

commit v2 on v1

v2 whole, which is shorter than its diff:
```python
import jax
import jax.numpy as jnp
from jax import lax
from jax.experimental import pallas as pl
from jax.experimental.pallas import tpu as pltpu
from jax.sharding import Mesh, PartitionSpec as P

scale_a = 0.7978845608
scale_b = 0.044715
BF = jnp.bfloat16
F32 = jnp.float32
ONE = 22
TWO = 8
BACK = 11


def gelu_and_slope(v):
    c = (scale_a * scale_b) * (v * v)
    t = jnp.tanh(v * (scale_a + c))
    p = 0.5 + 0.5 * t
    value = v * p
    slope = p + value * (scale_a + 3.0 * c) * (1.0 - t)
    return value, slope


def shifted(v, shift):
    rows = v.shape[1]
    h = lax.broadcasted_iota(jnp.int32, v.shape, 1)
    rolled = pltpu.roll(v, (-shift) % rows, 1)
    keep = (h < rows - shift) if shift > 0 else (h >= -shift)
    return jnp.where(keep, rolled, jnp.zeros_like(rolled))


def row_copies(v):
    v = v.astype(BF)
    z = jnp.zeros((v.shape[0], 2, v.shape[2]), BF)
    return jnp.concatenate([z, v[:, :-2]], axis=1), v, jnp.concatenate([v[:, 2:], z], axis=1)


def over_rows(a, b):
    return lax.dot_general(a, b, (((0,), (0,)), ((), ())), preferred_element_type=F32)


def block_kernel(
    place, low, middle, high, k1, k2, cot, fmap, keep, send,
    xe, taps, bottom, tail, hid, slope, delta, pairs2, pairs1, w1, w2, wb, acc2, acc1, total,
):
    zero = jnp.zeros((32, 128), BF)
    for k in range(6):
        for r in range(2):
            j = k - r
            for i in range(5):
                row = k * 128 + i * 32 if i < 4 else 768 + k * 32
                w1[row : row + 32, r * 128 : r * 128 + 128] = k1[i, j] if 0 <= j < 5 else zero
    w1[960:1024] = jnp.zeros((64, 256), BF)
    square = jnp.zeros((128, 128), BF)
    for i in range(3):
        for s in range(2):
            lanes = slice(s * 128, s * 128 + 128)
            for k in range(4):
                rows = slice((i * 4 + k) * 128, (i * 4 + k) * 128 + 128)
                j = k - s
                w2[rows, lanes] = k2[i, j] if 0 <= j < 3 else square
                j = s + 2 - k
                wb[rows, lanes] = k2[i, j].T if 0 <= j < 3 else square

    xe[0:4] = low[...]
    xe[4:132] = middle[...]
    xe[132:136] = high[...]
    bottom[136:140] = jnp.zeros((4, 32, 128), BF)

    def row_taps(n, carry):
        at = pl.ds(n * 34, 34)
        v = xe[at].astype(F32)
        lane = lax.broadcasted_iota(jnp.int32, v.shape, 2)
        taps[at] = jnp.where(
            lane < 64,
            jnp.where(lane < 32, shifted(v, -2), shifted(v, -1)),
            jnp.where(lane < 96, v, shifted(v, 1)),
        ).astype(BF)
        bottom[at] = shifted(v, 2).astype(BF)
        return carry

    lax.fori_loop(0, 4, row_taps, 0)
    lane = lax.broadcasted_iota(jnp.int32, (32, 128), 1)
    for v in range(68):
        s = [bottom[2 * v + k] for k in range(4)]
        tail[v] = jnp.where(
            lane < 64, jnp.where(lane < 32, s[0], s[1]), jnp.where(lane < 96, s[2], s[3])
        )

    def windows_one(v, n):
        parts = [jnp.concatenate([taps[2 * (v + t) + k] for t in range(n)], 0) for k in range(6)]
        parts += [tail[pl.ds(v + d, n)].reshape(n * 32, 128) for d in (0, 2)]
        return jnp.concatenate(parts, axis=1)

    def windows_two(ref, q, n):
        parts = [
            jnp.concatenate([ref[i, 2 * (q + t) + k] for t in range(n)], 0)
            for i in range(3)
            for k in range(4)
        ]
        return jnp.concatenate(parts, axis=1)

    def first(m, carry):
        v = m * ONE
        pre = jnp.dot(windows_one(v, ONE), w1[...], preferred_element_type=F32)
        for r in range(2):
            h, s = gelu_and_slope(pre[:, r * 128 : r * 128 + 128].reshape(ONE, 32, 128))
            at = (pl.ds(v, ONE), slice(r * 32, r * 32 + 32))
            slope[at] = s
            for i, copy in enumerate(row_copies(h)):
                hid[(i,) + at] = copy
        return carry

    lax.fori_loop(0, 66 // ONE, first, 0)

    @pl.when(place[0] == 0)
    def _():
        hid[:, 0] = jnp.zeros((3, 64, 128), BF)
        slope[0] = jnp.zeros((64, 128), F32)

    @pl.when(place[1] == 0)
    def _():
        hid[:, 65] = jnp.zeros((3, 64, 128), BF)
        slope[65] = jnp.zeros((64, 128), F32)

    delta[:, 0:2] = jnp.zeros((3, 2, 64, 128), BF)
    delta[:, 66:68] = jnp.zeros((3, 2, 64, 128), BF)

    def second(m, carry):
        q = m * TWO
        pre = jnp.dot(windows_two(hid, q, TWO), w2[...], preferred_element_type=F32)
        for s in range(2):
            f, sl = gelu_and_slope(pre[:, s * 128 : s * 128 + 128].reshape(TWO, 64, 128))
            fmap[pl.ds(q, TWO), s] = f.astype(BF)
            d = cot[pl.ds(q, TWO), s].astype(F32) * sl
            pairs2[pl.ds(q, TWO), :, s * 128 : s * 128 + 128] = d.astype(BF)
            for i, copy in enumerate(reversed(row_copies(d.reshape(TWO * 2, 32, 128)))):
                copy = copy.reshape(TWO, 64, 128)
                for t in range(TWO):
                    delta[i, 2 * (q + t) + 2 + s] = copy[t]
        return carry

    lax.fori_loop(0, 32 // TWO, second, 0)
    acc2[...] = over_rows(pairs2[...].reshape(2048, 256), windows_two(hid, 0, 32))

    def back(m, carry):
        q = m * BACK
        both = jnp.dot(windows_two(delta, q, BACK), wb[...], preferred_element_type=F32)
        for s in range(2):
            b = both[:, s * 128 : s * 128 + 128].reshape(BACK, 64, 128)
            for t in range(BACK):
                v = 2 * (q + t) + s
                d = (b[t] * slope[v]).astype(BF)
                pairs1[v, :, 0:128] = d[0:32]
                pairs1[v, :, 128:256] = d[32:64]
        return carry

    lax.fori_loop(0, 33 // BACK, back, 0)
    acc1[...] = over_rows(pairs1[...].reshape(2112, 256), windows_one(0, 66))

    for i in range(3):
        for j in range(3):
            at = (i * 4 + j) * 128
            to = (i * 3 + j) * 128
            both = acc2[0:128, at : at + 128] + acc2[128:256, at + 128 : at + 256]
            total[to : to + 128] = both.T
    for j in range(5):
        at = j * 128
        both = (acc1[0:128, at : at + 128] + acc1[128:256, at + 128 : at + 256]).T
        for i in range(4):
            to = 1152 + (i * 5 + j) * 32
            total[to : to + 32] = both[i * 32 : i * 32 + 32]
    even = acc1[0:128, 768:1024].T
    odd = acc1[128:256, 768:1024].T
    total[1792:1952] = even[0:160] + odd[32:192]
    total[1952:2048] = jnp.zeros((96, 128), F32)
    mine = pl.multiple_of(place[2] * 1024, 1024)
    other = pl.multiple_of((1 - place[2]) * 1024, 1024)
    keep[...] = total[pl.ds(mine, 1024)]
    send[...] = total[pl.ds(other, 1024)].astype(BF)


def block(place, low, middle, high, k1, k2, cot):
    vmem = pl.BlockSpec(memory_space=pltpu.VMEM)
    return pl.pallas_call(
        block_kernel,
        out_shape=(
            jax.ShapeDtypeStruct((32, 2, 64, 128), BF),
            jax.ShapeDtypeStruct((1024, 128), F32),
            jax.ShapeDtypeStruct((1024, 128), BF),
        ),
        in_specs=[pl.BlockSpec(memory_space=pltpu.SMEM)] + [vmem] * 6,
        out_specs=(vmem, vmem, vmem),
        scratch_shapes=[
            pltpu.VMEM((136, 32, 128), BF),
            pltpu.VMEM((136, 32, 128), BF),
            pltpu.VMEM((140, 32, 128), BF),
            pltpu.VMEM((68, 32, 128), BF),
            pltpu.VMEM((3, 66, 64, 128), BF),
            pltpu.VMEM((66, 64, 128), F32),
            pltpu.VMEM((3, 68, 64, 128), BF),
            pltpu.VMEM((32, 64, 256), BF),
            pltpu.VMEM((66, 32, 256), BF),
            pltpu.VMEM((1024, 256), BF),
            pltpu.VMEM((1536, 256), BF),
            pltpu.VMEM((1536, 256), BF),
            pltpu.VMEM((256, 1536), F32),
            pltpu.VMEM((256, 1024), F32),
            pltpu.VMEM((2048, 128), F32),
        ],
        compiler_params=pltpu.CompilerParams(vmem_limit_bytes=45 * 1024 * 1024),
        cost_estimate=pl.CostEstimate(
            flops=5_500_000_000, bytes_accessed=5_000_000, transcendentals=1_100_000
        ),
    )(place, low, middle, high, k1, k2, cot.reshape(32, 2, 64, 128))


def columns_first(block_of):
    return jnp.transpose(block_of[0], (2, 1, 0))


def fourfold(v):
    return jnp.tile(v, (1, 1, 4))


TRACK = ("y", "zh")
REP = ("x", "zl", "core")


def exchange(pieces, axes):
    return lax.all_to_all(pieces, axes, 0, 0, tiled=True)


def gathered(piece, axes, count):
    return exchange(jnp.broadcast_to(piece[None], (count,) + piece.shape), axes)


def summed(pieces):
    return jnp.sum(pieces.astype(F32), axis=0).astype(BF)


def on_device(features, kernel_one, kernel_two, cotangent):
    at = lax.axis_index(TRACK)
    core = lax.axis_index("core")
    up = [(i, i + 1) for i in range(15)]
    down = [(i + 1, i) for i in range(15)]
    middle = fourfold(columns_first(features))
    low = lax.ppermute(middle[124:], TRACK, up)
    high = lax.ppermute(middle[:4], TRACK, down)
    place = jnp.stack([(at > 0).astype(jnp.int32), (at < 15).astype(jnp.int32), core])
    fmap, keep, send = block(
        place, low, middle, high, kernel_one, kernel_two, columns_first(cotangent)
    )
    feature_map = jnp.transpose(fmap.reshape(128, 32, 128), (2, 1, 0))[None]
    swap = [(0, 1), (1, 0)]
    chip_sum = (keep + lax.ppermute(send, "core", swap).astype(F32)).astype(BF)
    layer_sum = summed(exchange(chip_sum.reshape(16, 64, 128), ("x", "y")))
    full_sum = summed(gathered(layer_sum, ("zh", "zl"), 8))
    half = gathered(full_sum, ("x", "y"), 16).reshape(1024, 128)
    rest = lax.ppermute(half, "core", swap)
    rows = jnp.concatenate(
        [jnp.where(core == 0, half, rest), jnp.where(core == 0, rest, half)], axis=0
    ).astype(F32)
    grad_two = rows[:1152].reshape(3, 3, 128, 128)
    grad_one = rows[1152:1952].reshape(5, 5, 32, 128)
    return (feature_map, grad_one, grad_two)


def solution(mesh):
    fine = Mesh(mesh.devices.reshape(4, 4, 4, 2, 2), TRACK + REP)
    placed = (P(REP, None, None, TRACK), P(), P(), P(REP, None, None, TRACK))
    return jax.shard_map(
        on_device,
        mesh=fine,
        in_specs=placed,
        out_specs=(P(REP, None, None, TRACK), P(), P()),
        check_vma=False,
    )
```

time: 101 us -> 82.6 us (0.82)
  Pallas kernels: 25.7 us -> 13.7 us
  blocking collectives: 48.7 us -> 39.1 us
  waiting for transfers between devices: 1.17 us -> 3.58 us
  starting transfers between devices: 11.9 us -> 13.3 us
    pallas_call x1, Pallas kernels: 25.7 us -> 13.7 us  [block(): pl.pallas_call(block_kernel, out_shape=(jax.ShapeDtypeStruct((32, 2, 64,...]
    all_to_all x2 -> x3, blocking collectives: 48.7 us -> 39.1 us  [exchange(): return lax.all_to_all(pieces, axes, 0, 0, tiled=True)]
    unnamed x8 -> x6, local copies, waits for them, and re-layouts: 6.21 us -> 0.94 us
    ppermute x2, waiting for transfers between devices: 0.01 us -> 2.42 us  [the longest x1 2.42 us: on_device(): high = lax.ppermute(middle[:4], TRACK, down)]
    reshape x0 -> x1, local copies, waits for them, and re-layouts: none -> 2.24 us  [on_device(): feature_map = jnp.transpose(fmap.reshape(128, 32, 128), (2, 1, 0))[None]]
    slice x2 -> x3, local copies, waits for them, and re-layouts: 0.66 us -> 1.96 us  [the longest x2 1.56 us: on_device(): high = lax.ppermute(middle[:4], TRACK, down)]
    transpose x4 -> x2, local copies, waits for them, and re-layouts: 2.07 us -> 2.63 us  [columns_first(): return jnp.transpose(block_of[0], (2, 1, 0))]
  transfers between devices with their start and end apart: 4 -> 4, of which waited for: 1 -> 2; matrix products, arithmetic and copies ran while one was open for 8% -> 9% of each run, Pallas kernels for 0% -> 0%
where the time goes in v2:
time: 82.6 us; the launch traced here: 82.3 us
  blocking collectives  39.1 us (47%)
  Pallas kernels  13.7 us (17%)
  starting transfers between devices  13.3 us (16%)
  local copies, waits for them, and re-layouts  9.91 us (12%)
  waiting for transfers between devices  3.58 us (4%)
  other arithmetic  1.89 us (2%)
    all_to_all x3, blocking collectives, exchange(): return lax.all_to_all(pieces, axes, 0, 0, tiled=True)  39.1 us
    pallas_call x1, Pallas kernels, block(): pl.pallas_call(block_kernel, out_shape=(jax.ShapeDtypeStruct((32, 2, 64,...  13.7 us
    ppermute x1, starting transfers between devices, on_device(): low = lax.ppermute(middle[124:], TRACK, up)  5.73 us
    ppermute x1, starting transfers between devices, on_device(): rest = lax.ppermute(half, 'core', swap)  4.38 us
    transpose x2, local copies, waits for them, and re-layouts, columns_first(): return jnp.transpose(block_of[0], (2, 1, 0))  2.63 us
    ppermute x1, waiting for transfers between devices, on_device(): high = lax.ppermute(middle[:4], TRACK, down)  2.42 us
    reshape x1, local copies, waits for them, and re-layouts, on_device(): feature_map = jnp.transpose(fmap.reshape(128, 32, 128), (2, 1, 0))[None]  2.24 us
    another operation x6, local copies, waits for them, and re-layouts, fourfold(): return jnp.tile(v, (1, 1, 4))  2.07 us
  transfers between devices with their start and end apart: 4, of which 2 were waited for; matrix products, arithmetic and copies ran while one was open for 9% of the time, Pallas kernels for 0%

profile of v2, /device:TPU:1, one launch (start us, length us, event | category | flops | bytes accessed | tf_op | source)
XLA Modules:
  0.0 82.3 jit_solution(6903735259226448831)
XLA Ops:
  0.6 1.2 %fusion.1 = (bf16[4,32,32]{0,1,2:T(8,128)(2,1)S(1)}, bf16[4,32,32]{0,1,2:T(8,128)(2,1)S(1)}) fusion(bf16[128,32,32]{0,1,2:T(8,128)(2,1)} %bitcast.24), kind=kLoop, calls=%fused_computation.7 | loop fusion | bytes 32768 | tf_op jit(solution)/shard_map/slice | solution.py:251
  1.8 0.4 copy.18
  2.2 0.1 tile.18
  2.4 5.7 %collective-permute-start = (bf16[4,32,128]{2,1,0:T(8,128)(2,1)S(1)}, bf16[4,32,128]{2,1,0:T(8,128)(2,1)S(1)}, u32[]{:S(2)}, u32[]{:S(2)}) collective-permute-start(bf16[4,32,128]{2,1,0:T(8,128)(2,1)S(1)} %tile.18), channel_id=1, source_target_pairs={{0,16},{16,32},{32,48},{48,64},{64,80},{80,96},{96,112},{112,128},... | collective-permute-start | bytes 98312 | tf_op jit(solution)/shard_map/ppermute | solution.py:250
  8.1 0.0 copy-start.2
  8.1 0.4 copy.20
  8.6 0.7 tile.22
  9.3 1.3 %collective-permute-start.1 = (bf16[4,32,128]{2,1,0:T(8,128)(2,1)}, bf16[4,32,128]{2,1,0:T(8,128)(2,1)S(1)}, u32[]{:S(2)}, u32[]{:S(2)}) collective-permute-start(bf16[4,32,128]{2,1,0:T(8,128)(2,1)} %tile.22), channel_id=1, source_target_pairs={{16,0},{32,16},{48,32},{64,48},{80,64},{96,80},{112,96},{128,112},... | collective-permute-start | bytes 98312 | tf_op jit(solution)/shard_map/ppermute | solution.py:251
  10.6 0.1 pad_add_fusion.place
  10.7 0.0 copy-done.2
  10.7 0.1 copy.19
  10.8 0.2 tile.19
  11.0 1.0 %copy.22.middle = bf16[128,32,128]{2,1,0:T(8,128)(2,1)S(1)} copy(bf16[128,32,128]{0,2,1:T(8,128)(2,1)S(1)} %bitcast.23) | data formatting | bytes 2097152 | tf_op jit(solution)/shard_map/tile | solution.py:225
  11.9 0.0 copy-start
  12.0 2.5 %copy.21 = bf16[128,32,128]{2,1,0:T(8,128)(2,1)S(1)} copy(bf16[128,32,128]{0,1,2:T(8,128)(2,1)} %bitcast.26) | data formatting | bytes 2097152 | tf_op jit(solution)/shard_map/transpose | solution.py:221
  14.5 0.0 collective-permute-done.low
  14.5 2.4 %collective-permute-done.1.high = bf16[4,32,128]{2,1,0:T(8,128)(2,1)S(1)} collective-permute-done((bf16[4,32,128]{2,1,0:T(8,128)(2,1)}, bf16[4,32,128]{2,1,0:T(8,128)(2,1)S(1)}, u32[]{:S(2)}, u32[]{:S(2)}) %collective-permute-start.1) | collective-permute-done | bytes 32800 | tf_op jit(solution)/shard_map/ppermute | solution.py:251
  16.9 0.0 copy-done
  16.9 0.9 %copy-done.1 = bf16[5,5,32,128]{3,2,1,0:T(8,128)(2,1)S(1)} copy-done((bf16[5,5,32,128]{3,2,1,0:T(8,128)(2,1)S(1)}, bf16[5,5,32,128]{3,2,1,0:T(8,128)(2,1)}, u32[]{:S(2)}) %copy-start.1) | copy-done | bytes 204824
  17.8 13.7 %shard_map.67 = (bf16[32,2,64,128]{3,2,1,0:T(8,128)(2,1)S(1)}, f32[1024,128]{1,0:T(8,128)S(1)}, bf16[1024,128]{1,0:T(8,128)(2,1)S(1)}) custom-call(s32[3]{0:T(128)S(1)} %pad_add_fusion.place, bf16[4,32,128]{2,1,0:T(8,128)(2,1)S(1)} %collective-permute-done.low, bf16[128,32,128]{2,1,0:T(8,128)(2,1)S(1)} %copy.22.middle, ...), custom_call_target="tpu_custom_call" | custom-call | flops 5500000256 | bytes 5000000 | tf_op jit(solution)/shard_map/pallas_call | solution.py:187
  31.6 1.9 %collective-permute-start.2 = (bf16[1024,128]{1,0:T(8,128)(2,1)S(1)}, bf16[1024,128]{1,0:T(8,128)(2,1)S(1)}, u32[]{:S(2)}, u32[]{:S(2)}) collective-permute-start(bf16[1024,128]{1,0:T(8,128)(2,1)S(1)} %get-tuple-element.8), channel_id=1, source_target_pairs={{0,1},{1,0},{2,3},{3,2},{4,5},{5,4},{6,7},{7,6},{8,9},{9,8},{10,11... | collective-permute-start | bytes 786440 | tf_op jit(solution)/shard_map/ppermute | solution.py:258
  33.5 1.2 %collective-permute-done.2 = bf16[1024,128]{1,0:T(8,128)(2,1)S(1)} collective-permute-done((bf16[1024,128]{1,0:T(8,128)(2,1)S(1)}, bf16[1024,128]{1,0:T(8,128)(2,1)S(1)}, u32[]{:S(2)}, u32[]{:S(2)}) %collective-permute-start.2) | collective-permute-done | bytes 262176 | tf_op jit(solution)/shard_map/ppermute | solution.py:258
  34.7 0.1 add_convert_fusion
  34.7 14.5 %all_to_all.15 = bf16[16,64,128]{2,1,0:T(8,128)(2,1)S(1)} all-to-all(bf16[16,64,128]{2,1,0:T(8,128)(2,1)S(1)} %bitcast.29), channel_id=1, replica_groups=mesh['y'=4,'zh'=4,'x'=4,'zl'=2,'core'=2] {'x','y'}, dimensions={0} | all-to-all | bytes 524288 | tf_op jit(solution)/shard_map/all_to_all | solution.py:233
  49.3 13.8 %all_to_all.16 = bf16[8,64,128]{2,1,0:T(8,128)(2,1)S(1)} all-to-all(bf16[8,64,128]{2,1,0:T(8,128)(2,1)S(1)} %broadcast_in_dim.7), channel_id=1, replica_groups=mesh['y'=4,'zh'=4,'x'=4,'zl'=2,'core'=2] {'zh','zl'}, dimensions={0} | all-to-all | bytes 262144 | tf_op jit(solution)/shard_map/all_to_all | solution.py:233
  63.2 10.7 %all_to_all.17 = bf16[16,64,128]{2,1,0:T(8,128)(2,1)S(1)} all-to-all(bf16[16,64,128]{2,1,0:T(8,128)(2,1)S(1)} %broadcast_in_dim.8), channel_id=1, replica_groups=mesh['y'=4,'zh'=4,'x'=4,'zl'=2,'core'=2] {'x','y'}, dimensions={0} | all-to-all | bytes 524288 | tf_op jit(solution)/shard_map/all_to_all | solution.py:233
  74.0 4.4 %collective-permute-start.3 = (bf16[1024,128]{1,0:T(8,128)(2,1)S(1)}, bf16[1024,128]{1,0:T(8,128)(2,1)S(1)}, u32[]{:S(2)}, u32[]{:S(2)}) collective-permute-start(bf16[1024,128]{1,0:T(8,128)(2,1)S(1)} %bitcast.28), channel_id=1, source_target_pairs={{0,1},{1,0},{2,3},{3,2},{4,5},{5,4},{6,7},{7,6},{8,9},{9,8},{10,11... | collective-permute-start | bytes 786440 | tf_op jit(solution)/shard_map/ppermute | solution.py:262
  78.3 2.2 %copy.23 = bf16[128,32,128]{0,1,2:T(8,128)(2,1)} copy(bf16[128,32,128]{2,1,0:T(8,128)(2,1)S(1)} %bitcast.21) | data formatting | bytes 2097152 | tf_op jit(solution)/shard_map/reshape | solution.py:256
  80.6 0.0 collective-permute-done.3
  80.6 0.1 broadcast_select_fusion.1
  80.6 0.8 maximum_convert_fusion
  81.4 0.9 %fusion = f32[1152,128]{1,0:T(8,128)} fusion(bf16[1024,128]{1,0:T(8,128)(2,1)S(1)} %get-tuple-element.10, bf16[1024,128]{1,0:T(8,128)(2,1)S(1)} %get-tuple-element.9), kind=kLoop, calls=%fused_computation.2 | loop fusion | flops 589824 | bytes 1114112 | tf_op jit(solution)/shard_map/convert_element_type | solution.py:265
  (7 shorter events, 0.2 us)
Async XLA Ops:
  2.4 12.1 %collective-permute-start = (bf16[4,32,128]{2,1,0:T(8,128)(2,1)S(1)}, bf16[4,32,128]{2,1,0:T(8,128)(2,1)S(1)}, u32[]{:S(2)}, u32[]{:S(2)}) collective-permute-start(bf16[4,32,128]{2,1,0:T(8,128)(2,1)S(1)} %tile.18), channel_id=1, source_target_pairs={{0,16},{16,32},{32,48},{48,64},{64,80},{80,96},{96,112},{112,128},... | collective-permute-start | bytes 98312 | tf_op jit(solution)/shard_map/ppermute | solution.py:250
  8.1 2.6 %copy-start.2 = (bf16[1,32,32,128]{3,2,1,0:T(8,128)(2,1)S(1)}, bf16[1,32,32,128]{3,2,1,0:T(8,128)(2,1)}, u32[]{:S(2)}) copy-start(bf16[1,32,32,128]{3,2,1,0:T(8,128)(2,1)} %param.4) | copy-start | bytes 786436
  9.3 7.6 %collective-permute-start.1 = (bf16[4,32,128]{2,1,0:T(8,128)(2,1)}, bf16[4,32,128]{2,1,0:T(8,128)(2,1)S(1)}, u32[]{:S(2)}, u32[]{:S(2)}) collective-permute-start(bf16[4,32,128]{2,1,0:T(8,128)(2,1)} %tile.22), channel_id=1, source_target_pairs={{16,0},{32,16},{48,32},{64,48},{80,64},{96,80},{112,96},{128,112},... | collective-permute-start | bytes 98312 | tf_op jit(solution)/shard_map/ppermute | solution.py:251
  11.9 5.0 %copy-start = (bf16[3,3,128,128]{3,2,1,0:T(8,128)(2,1)S(1)}, bf16[3,3,128,128]{3,2,1,0:T(8,128)(2,1)}, u32[]{:S(2)}) copy-start(bf16[3,3,128,128]{3,2,1,0:T(8,128)(2,1)} %k2.1) | copy-start | bytes 884740
  16.9 0.9 %copy-start.1 = (bf16[5,5,32,128]{3,2,1,0:T(8,128)(2,1)S(1)}, bf16[5,5,32,128]{3,2,1,0:T(8,128)(2,1)}, u32[]{:S(2)}) copy-start(bf16[5,5,32,128]{3,2,1,0:T(8,128)(2,1)} %k1.1) | copy-start | bytes 614404
  31.6 3.1 %collective-permute-start.2 = (bf16[1024,128]{1,0:T(8,128)(2,1)S(1)}, bf16[1024,128]{1,0:T(8,128)(2,1)S(1)}, u32[]{:S(2)}, u32[]{:S(2)}) collective-permute-start(bf16[1024,128]{1,0:T(8,128)(2,1)S(1)} %get-tuple-element.8), channel_id=1, source_target_pairs={{0,1},{1,0},{2,3},{3,2},{4,5},{5,4},{6,7},{7,6},{8,9},{9,8},{10,11... | collective-permute-start | bytes 786440 | tf_op jit(solution)/shard_map/ppermute | solution.py:258
  74.0 6.6 %collective-permute-start.3 = (bf16[1024,128]{1,0:T(8,128)(2,1)S(1)}, bf16[1024,128]{1,0:T(8,128)(2,1)S(1)}, u32[]{:S(2)}, u32[]{:S(2)}) collective-permute-start(bf16[1024,128]{1,0:T(8,128)(2,1)S(1)} %bitcast.28), channel_id=1, source_target_pairs={{0,1},{1,0},{2,3},{3,2},{4,5},{5,4},{6,7},{7,6},{8,9},{9,8},{10,11... | collective-permute-start | bytes 786440 | tf_op jit(solution)/shard_map/ppermute | solution.py:262

commit v3 on v2

--- a/solution.py
+++ b/solution.py
@@ -9,9 +9,9 @@
 scale_b = 0.044715
 BF = jnp.bfloat16
 F32 = jnp.float32
-ONE = 22
-TWO = 8
-BACK = 11
+ONE = 6
+TWO = 2
+BACK = 3
 
 
 def gelu_and_slope(v):
@@ -113,7 +113,7 @@
                 hid[(i,) + at] = copy
         return carry
 
-    lax.fori_loop(0, 66 // ONE, first, 0)
+    lax.fori_loop(0, 66 // ONE, first, 0, unroll=True)
 
     @pl.when(place[0] == 0)
     def _():
@@ -142,7 +142,7 @@
                     delta[i, 2 * (q + t) + 2 + s] = copy[t]
         return carry
 
-    lax.fori_loop(0, 32 // TWO, second, 0)
+    lax.fori_loop(0, 32 // TWO, second, 0, unroll=True)
     acc2[...] = over_rows(pairs2[...].reshape(2048, 256), windows_two(hid, 0, 32))
 
     def back(m, carry):
@@ -157,7 +157,7 @@
                 pairs1[v, :, 128:256] = d[32:64]
         return carry
 
-    lax.fori_loop(0, 33 // BACK, back, 0)
+    lax.fori_loop(0, 33 // BACK, back, 0, unroll=True)
     acc1[...] = over_rows(pairs1[...].reshape(2112, 256), windows_one(0, 66))
 
     for i in range(3):
@@ -246,7 +246,7 @@
     core = lax.axis_index("core")
     up = [(i, i + 1) for i in range(15)]
     down = [(i + 1, i) for i in range(15)]
-    middle = fourfold(columns_first(features))
+    middle = lax.optimization_barrier(fourfold(columns_first(features)))
     low = lax.ppermute(middle[124:], TRACK, up)
     high = lax.ppermute(middle[:4], TRACK, down)
     place = jnp.stack([(at > 0).astype(jnp.int32), (at < 15).astype(jnp.int32), core])

time: 82.6 us -> 78.9 us (0.955)
  waiting for transfers between devices: 3.58 us -> 1.17 us
  Pallas kernels: 13.7 us -> 11.5 us
  blocking collectives: 39.1 us -> 41.2 us
  local copies, waits for them, and re-layouts: 9.91 us -> 7.95 us
    ppermute x1, waiting for transfers between devices: 2.42 us -> 0.01 us  [on_device(): high = lax.ppermute(middle[:4], TRACK, down)]
    pallas_call x1, Pallas kernels: 13.7 us -> 11.5 us  [block(): pl.pallas_call(block_kernel, out_shape=(jax.ShapeDtypeStruct((32, 2, 64,...]
    all_to_all x3, blocking collectives: 39.1 us -> 41.2 us  [exchange(): return lax.all_to_all(pieces, axes, 0, 0, tiled=True)]
    another operation x6 -> x1, local copies, waits for them, and re-layouts: 2.07 us -> 0.16 us  [fourfold(): return jnp.tile(v, (1, 1, 4))]
    slice x2 -> x1, local copies, waits for them, and re-layouts: 1.56 us -> 0.01 us  [on_device(): high = lax.ppermute(middle[:4], TRACK, down)]
    optimization_barrier x0 -> x1, local copies, waits for them, and re-layouts: none -> 0.98 us  [on_device(): middle = lax.optimization_barrier(fourfold(columns_first(features)))]
    transpose x2, local copies, waits for them, and re-layouts: 2.63 us -> 3.57 us  [columns_first(): return jnp.transpose(block_of[0], (2, 1, 0))]
  transfers between devices with their start and end apart: 4 -> 4, of which waited for: 2 -> 1; matrix products, arithmetic and copies ran while one was open for 9% -> 6% of each run, Pallas kernels for 0% -> 0%
where the time goes in v3:
time: 78.9 us; the launch traced here: 78.6 us
  blocking collectives  41.2 us (52%)
  starting transfers between devices  14.1 us (18%)
  Pallas kernels  11.5 us (15%)
  local copies, waits for them, and re-layouts  7.95 us (10%)
  other arithmetic  1.89 us (2%)
  waiting for transfers between devices  1.17 us (1%)
    all_to_all x3, blocking collectives, exchange(): return lax.all_to_all(pieces, axes, 0, 0, tiled=True)  41.2 us
    pallas_call x1, Pallas kernels, block(): pl.pallas_call(block_kernel, out_shape=(jax.ShapeDtypeStruct((32, 2, 64,...  11.5 us
    ppermute x1, starting transfers between devices, on_device(): low = lax.ppermute(middle[124:], TRACK, up)  6.35 us
    ppermute x1, starting transfers between devices, on_device(): rest = lax.ppermute(half, 'core', swap)  4.06 us
    transpose x2, local copies, waits for them, and re-layouts, columns_first(): return jnp.transpose(block_of[0], (2, 1, 0))  3.57 us
    ppermute x1, starting transfers between devices, on_device(): chip_sum = (keep + lax.ppermute(send, 'core', swap).astype(F32)).astype(BF)  2.42 us
    reshape x1, local copies, waits for them, and re-layouts, on_device(): feature_map = jnp.transpose(fmap.reshape(128, 32, 128), (2, 1, 0))[None]  2.24 us
  transfers between devices with their start and end apart: 4, of which 1 were waited for; matrix products, arithmetic and copies ran while one was open for 6% of the time, Pallas kernels for 0%

profile of v3, /device:TPU:1, one launch (start us, length us, event | category | flops | bytes accessed | tf_op | source)
XLA Modules:
  0.0 78.6 jit_solution(11815201276386384157)
XLA Ops:
  0.6 1.1 %copy.16 = bf16[128,32,32]{0,2,1:T(8,128)(2,1)S(1)} copy(bf16[128,32,32]{0,1,2:T(8,128)(2,1)} %bitcast.30) | data formatting | bytes 524288 | tf_op jit(solution)/shard_map/transpose | solution.py:221
  1.7 0.2 tile.4
  1.9 1.0 %copy.17.middle = bf16[128,32,128]{2,1,0:T(8,128)(2,1)S(1)} copy(bf16[128,32,128]{0,2,1:T(8,128)(2,1)S(1)} %bitcast.23) | data formatting | bytes 2097152 | tf_op jit(solution)/shard_map/optimization_barrier | solution.py:249
  2.9 1.3 %collective-permute-start.1 = (bf16[4,32,128]{2,1,0:T(8,128)(2,1)S(1)}, bf16[4,32,128]{2,1,0:T(8,128)(2,1)S(1)}, u32[]{:S(2)}, u32[]{:S(2)}) collective-permute-start(bf16[4,32,128]{2,1,0:T(8,128)(2,1)S(1)} %get-tuple-element.9), channel_id=1, source_target_pairs={{16,0},{32,16},{48,32},{64,48},{80,64},{96,80},{112,96},{128,112},... | collective-permute-start | bytes 98312 | tf_op jit(solution)/shard_map/ppermute | solution.py:251
  4.2 6.4 %collective-permute-start = (bf16[4,32,128]{2,1,0:T(8,128)(2,1)S(1)}, bf16[4,32,128]{2,1,0:T(8,128)(2,1)S(1)}, u32[]{:S(2)}, u32[]{:S(2)}) collective-permute-start(bf16[4,32,128]{2,1,0:T(8,128)(2,1)S(1)} %get-tuple-element.10), channel_id=1, source_target_pairs={{0,16},{16,32},{32,48},{48,64},{64,80},{80,96},{96,112},{112,128},... | collective-permute-start | bytes 98312 | tf_op jit(solution)/shard_map/ppermute | solution.py:250
  10.5 0.1 pad_add_fusion.place
  10.6 0.0 copy-start
  10.6 2.5 %copy.19 = bf16[128,32,128]{2,1,0:T(8,128)(2,1)S(1)} copy(bf16[128,32,128]{0,1,2:T(8,128)(2,1)} %bitcast.24) | data formatting | bytes 2097152 | tf_op jit(solution)/shard_map/transpose | solution.py:221
  13.1 0.0 collective-permute-done.1.high
  13.1 0.0 collective-permute-done.low
  13.1 0.0 copy-done
  13.2 0.0 copy-start.1
  13.2 0.9 %copy-done.1 = bf16[5,5,32,128]{3,2,1,0:T(8,128)(2,1)S(1)} copy-done((bf16[5,5,32,128]{3,2,1,0:T(8,128)(2,1)S(1)}, bf16[5,5,32,128]{3,2,1,0:T(8,128)(2,1)}, u32[]{:S(2)}) %copy-start.1) | copy-done | bytes 204824
  14.1 11.5 %shard_map.67 = (bf16[32,2,64,128]{3,2,1,0:T(8,128)(2,1)S(1)}, f32[1024,128]{1,0:T(8,128)S(1)}, bf16[1024,128]{1,0:T(8,128)(2,1)S(1)}) custom-call(s32[3]{0:T(128)S(1)} %pad_add_fusion.place, bf16[4,32,128]{2,1,0:T(8,128)(2,1)S(1)} %collective-permute-done.low, bf16[128,32,128]{2,1,0:T(8,128)(2,1)S(1)} %copy.17.middle, ...), custom_call_target="tpu_custom_call" | custom-call | flops 5500000256 | bytes 5000000 | tf_op jit(solution)/shard_map/pallas_call | solution.py:187
  25.6 2.4 %collective-permute-start.2 = (bf16[1024,128]{1,0:T(8,128)(2,1)S(1)}, bf16[1024,128]{1,0:T(8,128)(2,1)S(1)}, u32[]{:S(2)}, u32[]{:S(2)}) collective-permute-start(bf16[1024,128]{1,0:T(8,128)(2,1)S(1)} %get-tuple-element.8), channel_id=1, source_target_pairs={{0,1},{1,0},{2,3},{3,2},{4,5},{5,4},{6,7},{7,6},{8,9},{9,8},{10,11... | collective-permute-start | bytes 786440 | tf_op jit(solution)/shard_map/ppermute | solution.py:258
  28.0 1.2 %collective-permute-done.2 = bf16[1024,128]{1,0:T(8,128)(2,1)S(1)} collective-permute-done((bf16[1024,128]{1,0:T(8,128)(2,1)S(1)}, bf16[1024,128]{1,0:T(8,128)(2,1)S(1)}, u32[]{:S(2)}, u32[]{:S(2)}) %collective-permute-start.2) | collective-permute-done | bytes 262176 | tf_op jit(solution)/shard_map/ppermute | solution.py:258
  29.2 0.1 add_convert_fusion
  29.3 20.0 %all_to_all.15 = bf16[16,64,128]{2,1,0:T(8,128)(2,1)S(1)} all-to-all(bf16[16,64,128]{2,1,0:T(8,128)(2,1)S(1)} %bitcast.27), channel_id=1, replica_groups=mesh['y'=4,'zh'=4,'x'=4,'zl'=2,'core'=2] {'x','y'}, dimensions={0} | all-to-all | bytes 524288 | tf_op jit(solution)/shard_map/all_to_all | solution.py:233
  49.4 10.4 %all_to_all.16 = bf16[8,64,128]{2,1,0:T(8,128)(2,1)S(1)} all-to-all(bf16[8,64,128]{2,1,0:T(8,128)(2,1)S(1)} %broadcast_in_dim.7), channel_id=1, replica_groups=mesh['y'=4,'zh'=4,'x'=4,'zl'=2,'core'=2] {'zh','zl'}, dimensions={0} | all-to-all | bytes 262144 | tf_op jit(solution)/shard_map/all_to_all | solution.py:233
  59.8 10.8 %all_to_all.17 = bf16[16,64,128]{2,1,0:T(8,128)(2,1)S(1)} all-to-all(bf16[16,64,128]{2,1,0:T(8,128)(2,1)S(1)} %broadcast_in_dim.8), channel_id=1, replica_groups=mesh['y'=4,'zh'=4,'x'=4,'zl'=2,'core'=2] {'x','y'}, dimensions={0} | all-to-all | bytes 524288 | tf_op jit(solution)/shard_map/all_to_all | solution.py:233
  70.6 4.1 %collective-permute-start.3 = (bf16[1024,128]{1,0:T(8,128)(2,1)S(1)}, bf16[1024,128]{1,0:T(8,128)(2,1)S(1)}, u32[]{:S(2)}, u32[]{:S(2)}) collective-permute-start(bf16[1024,128]{1,0:T(8,128)(2,1)S(1)} %bitcast.26), channel_id=1, source_target_pairs={{0,1},{1,0},{2,3},{3,2},{4,5},{5,4},{6,7},{7,6},{8,9},{9,8},{10,11... | collective-permute-start | bytes 786440 | tf_op jit(solution)/shard_map/ppermute | solution.py:262
  74.7 2.2 %copy.21 = bf16[128,32,128]{0,1,2:T(8,128)(2,1)} copy(bf16[128,32,128]{2,1,0:T(8,128)(2,1)S(1)} %bitcast.21) | data formatting | bytes 2097152 | tf_op jit(solution)/shard_map/reshape | solution.py:256
  76.9 0.0 collective-permute-done.3
  76.9 0.1 broadcast_select_fusion.1
  77.0 0.8 maximum_convert_fusion
  77.8 0.9 %fusion = f32[1152,128]{1,0:T(8,128)} fusion(bf16[1024,128]{1,0:T(8,128)(2,1)S(1)} %get-tuple-element.12, bf16[1024,128]{1,0:T(8,128)(2,1)S(1)} %get-tuple-element.11), kind=kLoop, calls=%fused_computation.2 | loop fusion | flops 589824 | bytes 1114112 | tf_op jit(solution)/shard_map/convert_element_type | solution.py:265
  (5 shorter events, 0.1 us)
Async XLA Ops:
  2.9 10.3 %collective-permute-start.1 = (bf16[4,32,128]{2,1,0:T(8,128)(2,1)S(1)}, bf16[4,32,128]{2,1,0:T(8,128)(2,1)S(1)}, u32[]{:S(2)}, u32[]{:S(2)}) collective-permute-start(bf16[4,32,128]{2,1,0:T(8,128)(2,1)S(1)} %get-tuple-element.9), channel_id=1, source_target_pairs={{16,0},{32,16},{48,32},{64,48},{80,64},{96,80},{112,96},{128,112},... | collective-permute-start | bytes 98312 | tf_op jit(solution)/shard_map/ppermute | solution.py:251
  4.2 9.0 %collective-permute-start = (bf16[4,32,128]{2,1,0:T(8,128)(2,1)S(1)}, bf16[4,32,128]{2,1,0:T(8,128)(2,1)S(1)}, u32[]{:S(2)}, u32[]{:S(2)}) collective-permute-start(bf16[4,32,128]{2,1,0:T(8,128)(2,1)S(1)} %get-tuple-element.10), channel_id=1, source_target_pairs={{0,16},{16,32},{32,48},{48,64},{64,80},{80,96},{96,112},{112,128},... | collective-permute-start | bytes 98312 | tf_op jit(solution)/shard_map/ppermute | solution.py:250
  10.6 2.5 %copy-start = (bf16[3,3,128,128]{3,2,1,0:T(8,128)(2,1)S(1)}, bf16[3,3,128,128]{3,2,1,0:T(8,128)(2,1)}, u32[]{:S(2)}) copy-start(bf16[3,3,128,128]{3,2,1,0:T(8,128)(2,1)} %k2.1) | copy-start | bytes 884740
  13.2 0.9 %copy-start.1 = (bf16[5,5,32,128]{3,2,1,0:T(8,128)(2,1)S(1)}, bf16[5,5,32,128]{3,2,1,0:T(8,128)(2,1)}, u32[]{:S(2)}) copy-start(bf16[5,5,32,128]{3,2,1,0:T(8,128)(2,1)} %k1.1) | copy-start | bytes 614404
  25.6 3.6 %collective-permute-start.2 = (bf16[1024,128]{1,0:T(8,128)(2,1)S(1)}, bf16[1024,128]{1,0:T(8,128)(2,1)S(1)}, u32[]{:S(2)}, u32[]{:S(2)}) collective-permute-start(bf16[1024,128]{1,0:T(8,128)(2,1)S(1)} %get-tuple-element.8), channel_id=1, source_target_pairs={{0,1},{1,0},{2,3},{3,2},{4,5},{5,4},{6,7},{7,6},{8,9},{9,8},{10,11... | collective-permute-start | bytes 786440 | tf_op jit(solution)/shard_map/ppermute | solution.py:258
  70.6 6.3 %collective-permute-start.3 = (bf16[1024,128]{1,0:T(8,128)(2,1)S(1)}, bf16[1024,128]{1,0:T(8,128)(2,1)S(1)}, u32[]{:S(2)}, u32[]{:S(2)}) collective-permute-start(bf16[1024,128]{1,0:T(8,128)(2,1)S(1)} %bitcast.26), channel_id=1, source_target_pairs={{0,1},{1,0},{2,3},{3,2},{4,5},{5,4},{6,7},{7,6},{8,9},{9,8},{10,11... | collective-permute-start | bytes 786440 | tf_op jit(solution)/shard_map/ppermute | solution.py:262

commit v4 on v3

--- a/solution.py
+++ b/solution.py
@@ -41,10 +41,7 @@
     return lax.dot_general(a, b, (((0,), (0,)), ((), ())), preferred_element_type=F32)
 
 
-def block_kernel(
-    place, low, middle, high, k1, k2, cot, fmap, keep, send,
-    xe, taps, bottom, tail, hid, slope, delta, pairs2, pairs1, w1, w2, wb, acc2, acc1, total,
-):
+def weights_kernel(k1, k2, w1, w2, wb):
     zero = jnp.zeros((32, 128), BF)
     for k in range(6):
         for r in range(2):
@@ -64,24 +61,39 @@
                 j = s + 2 - k
                 wb[rows, lanes] = k2[i, j].T if 0 <= j < 3 else square
 
-    xe[0:4] = low[...]
-    xe[4:132] = middle[...]
-    xe[132:136] = high[...]
+
+def weights(k1, k2):
+    vmem = pl.BlockSpec(memory_space=pltpu.VMEM)
+    return pl.pallas_call(
+        weights_kernel,
+        out_shape=(
+            jax.ShapeDtypeStruct((1024, 256), BF),
+            jax.ShapeDtypeStruct((1536, 256), BF),
+            jax.ShapeDtypeStruct((1536, 256), BF),
+        ),
+        in_specs=[vmem] * 2,
+        out_specs=(vmem,) * 3,
+        compiler_params=pltpu.CompilerParams(vmem_limit_bytes=8 * 1024 * 1024),
+        cost_estimate=pl.CostEstimate(flops=0, bytes_accessed=2_500_000, transcendentals=0),
+    )(k1, k2)
+
+
+def block_kernel(
+    place, low, middle, high, w1, w2, wb, cot, fmap, keep, send,
+    taps, bottom, tail, hid, slope, delta, pairs2, pairs1, acc2, acc1, total,
+):
     bottom[136:140] = jnp.zeros((4, 32, 128), BF)
-
-    def row_taps(n, carry):
-        at = pl.ds(n * 34, 34)
-        v = xe[at].astype(F32)
-        lane = lax.broadcasted_iota(jnp.int32, v.shape, 2)
+    lane = lax.broadcasted_iota(jnp.int32, (4, 32, 128), 2)
+    for n in range(34):
+        at = slice(n * 4, n * 4 + 4)
+        x = low[...] if n == 0 else high[...] if n == 33 else middle[n * 4 - 4 : n * 4]
+        v = x.astype(F32)
         taps[at] = jnp.where(
             lane < 64,
             jnp.where(lane < 32, shifted(v, -2), shifted(v, -1)),
             jnp.where(lane < 96, v, shifted(v, 1)),
         ).astype(BF)
-        bottom[at] = shifted(v, 2).astype(BF)
-        return carry
-
-    lax.fori_loop(0, 4, row_taps, 0)
+        bottom[at] = row_copies(x)[2]
     lane = lax.broadcasted_iota(jnp.int32, (32, 128), 1)
     for v in range(68):
         s = [bottom[2 * v + k] for k in range(4)]
@@ -182,7 +194,7 @@
     send[...] = total[pl.ds(other, 1024)].astype(BF)
 
 
-def block(place, low, middle, high, k1, k2, cot):
+def block(place, low, middle, high, w1, w2, wb, cot):
     vmem = pl.BlockSpec(memory_space=pltpu.VMEM)
     return pl.pallas_call(
         block_kernel,
@@ -191,10 +203,9 @@
             jax.ShapeDtypeStruct((1024, 128), F32),
             jax.ShapeDtypeStruct((1024, 128), BF),
         ),
-        in_specs=[pl.BlockSpec(memory_space=pltpu.SMEM)] + [vmem] * 6,
+        in_specs=[pl.BlockSpec(memory_space=pltpu.SMEM)] + [vmem] * 7,
         out_specs=(vmem, vmem, vmem),
         scratch_shapes=[
-            pltpu.VMEM((136, 32, 128), BF),
             pltpu.VMEM((136, 32, 128), BF),
             pltpu.VMEM((140, 32, 128), BF),
             pltpu.VMEM((68, 32, 128), BF),
@@ -203,9 +214,6 @@
             pltpu.VMEM((3, 68, 64, 128), BF),
             pltpu.VMEM((32, 64, 256), BF),
             pltpu.VMEM((66, 32, 256), BF),
-            pltpu.VMEM((1024, 256), BF),
-            pltpu.VMEM((1536, 256), BF),
-            pltpu.VMEM((1536, 256), BF),
             pltpu.VMEM((256, 1536), F32),
             pltpu.VMEM((256, 1024), F32),
             pltpu.VMEM((2048, 128), F32),
@@ -214,7 +222,7 @@
         cost_estimate=pl.CostEstimate(
             flops=5_500_000_000, bytes_accessed=5_000_000, transcendentals=1_100_000
         ),
-    )(place, low, middle, high, k1, k2, cot.reshape(32, 2, 64, 128))
+    )(place, low, middle, high, w1, w2, wb, cot.reshape(32, 2, 64, 128))
 
 
 def columns_first(block_of):
@@ -250,12 +258,12 @@
     low = lax.ppermute(middle[124:], TRACK, up)
     high = lax.ppermute(middle[:4], TRACK, down)
     place = jnp.stack([(at > 0).astype(jnp.int32), (at < 15).astype(jnp.int32), core])
-    fmap, keep, send = block(
-        place, low, middle, high, kernel_one, kernel_two, columns_first(cotangent)
-    )
+    cot = columns_first(cotangent)
+    fmap, keep, send = block(place, low, middle, high, *weights(kernel_one, kernel_two), cot)
+    swap = [(0, 1), (1, 0)]
+    sibling = lax.ppermute(send, "core", swap)
     feature_map = jnp.transpose(fmap.reshape(128, 32, 128), (2, 1, 0))[None]
-    swap = [(0, 1), (1, 0)]
-    chip_sum = (keep + lax.ppermute(send, "core", swap).astype(F32)).astype(BF)
+    chip_sum = (keep + sibling.astype(F32)).astype(BF)
     layer_sum = summed(exchange(chip_sum.reshape(16, 64, 128), ("x", "y")))
     full_sum = summed(gathered(layer_sum, ("zh", "zl"), 8))
     half = gathered(full_sum, ("x", "y"), 16).reshape(1024, 128)

time: 78.9 us -> 77.2 us (0.978)
  local copies, waits for them, and re-layouts: 7.95 us -> 7.04 us
    unnamed x4, local copies, waits for them, and re-layouts: 0.93 us -> 0.01 us
where the time goes in v4:
time: 77.2 us; the launch traced here: 76.9 us
  blocking collectives  40.8 us (53%)
  starting transfers between devices  14.1 us (18%)
  Pallas kernels  11.1 us (14%)
  local copies, waits for them, and re-layouts  7.04 us (9%)
  other arithmetic  1.89 us (2%)
  waiting for transfers between devices  1.17 us (2%)
    all_to_all x3, blocking collectives, exchange(): return lax.all_to_all(pieces, axes, 0, 0, tiled=True)  40.8 us
    pallas_call x1, Pallas kernels, block(): pl.pallas_call(block_kernel, out_shape=(jax.ShapeDtypeStruct((32, 2, 64,...  10.7 us
    ppermute x1, starting transfers between devices, on_device(): low = lax.ppermute(middle[124:], TRACK, up)  6.35 us
    ppermute x1, starting transfers between devices, on_device(): rest = lax.ppermute(half, 'core', swap)  4.06 us
    transpose x2, local copies, waits for them, and re-layouts, columns_first(): return jnp.transpose(block_of[0], (2, 1, 0))  3.58 us
    ppermute x1, starting transfers between devices, on_device(): sibling = lax.ppermute(send, 'core', swap)  2.42 us
    reshape x1, local copies, waits for them, and re-layouts, on_device(): feature_map = jnp.transpose(fmap.reshape(128, 32, 128), (2, 1, 0))[None]  2.24 us
  transfers between devices with their start and end apart: 4, of which 1 were waited for; matrix products, arithmetic and copies ran while one was open for 6% of the time, Pallas kernels for 0%

profile of v4, /device:TPU:1, one launch (start us, length us, event | category | flops | bytes accessed | tf_op | source)
XLA Modules:
  0.0 76.9 jit_solution(10754444353524216911)
XLA Ops:
  0.6 1.1 %copy.16 = bf16[128,32,32]{0,2,1:T(8,128)(2,1)S(1)} copy(bf16[128,32,32]{0,1,2:T(8,128)(2,1)} %bitcast.30) | data formatting | bytes 524288 | tf_op jit(solution)/shard_map/transpose | solution.py:229
  1.7 0.2 tile.4
  1.9 1.0 %copy.17.middle = bf16[128,32,128]{2,1,0:T(8,128)(2,1)S(1)} copy(bf16[128,32,128]{0,2,1:T(8,128)(2,1)S(1)} %bitcast.23) | data formatting | bytes 2097152 | tf_op jit(solution)/shard_map/optimization_barrier | solution.py:257
  2.9 1.3 %collective-permute-start.1 = (bf16[4,32,128]{2,1,0:T(8,128)(2,1)S(1)}, bf16[4,32,128]{2,1,0:T(8,128)(2,1)S(1)}, u32[]{:S(2)}, u32[]{:S(2)}) collective-permute-start(bf16[4,32,128]{2,1,0:T(8,128)(2,1)S(1)} %get-tuple-element.15), channel_id=1, source_target_pairs={{16,0},{32,16},{48,32},{64,48},{80,64},{96,80},{112,96},{128,112},... | collective-permute-start | bytes 98312 | tf_op jit(solution)/shard_map/ppermute | solution.py:259
  4.2 6.4 %collective-permute-start = (bf16[4,32,128]{2,1,0:T(8,128)(2,1)S(1)}, bf16[4,32,128]{2,1,0:T(8,128)(2,1)S(1)}, u32[]{:S(2)}, u32[]{:S(2)}) collective-permute-start(bf16[4,32,128]{2,1,0:T(8,128)(2,1)S(1)} %get-tuple-element.16), channel_id=1, source_target_pairs={{0,16},{16,32},{32,48},{48,64},{64,80},{80,96},{96,112},{112,128},... | collective-permute-start | bytes 98312 | tf_op jit(solution)/shard_map/ppermute | solution.py:258
  10.5 0.1 pad_add_fusion.place
  10.6 0.0 copy-start
  10.6 0.0 copy-start.1
  10.6 2.5 %copy.19 = bf16[128,32,128]{2,1,0:T(8,128)(2,1)S(1)} copy(bf16[128,32,128]{0,1,2:T(8,128)(2,1)} %bitcast.24) | data formatting | bytes 2097152 | tf_op jit(solution)/shard_map/transpose | solution.py:229
  13.1 0.0 copy-done
  13.2 0.0 copy-done.1
  13.2 0.4 shard_map.67
  13.5 0.0 collective-permute-done.1.high
  13.5 0.0 collective-permute-done.low
  13.5 10.7 %shard_map.68 = (bf16[32,2,64,128]{3,2,1,0:T(8,128)(2,1)S(1)}, f32[1024,128]{1,0:T(8,128)S(1)}, bf16[1024,128]{1,0:T(8,128)(2,1)S(1)}) custom-call(s32[3]{0:T(128)S(1)} %pad_add_fusion.place, bf16[4,32,128]{2,1,0:T(8,128)(2,1)S(1)} %collective-permute-done.low, bf16[128,32,128]{2,1,0:T(8,128)(2,1)S(1)} %copy.17.middle, ...), custom_call_target="tpu_custom_call" | custom-call | flops 5500000256 | bytes 5000000 | tf_op jit(solution)/shard_map/pallas_call | solution.py:199
  24.3 2.4 %collective-permute-start.2 = (bf16[1024,128]{1,0:T(8,128)(2,1)S(1)}, bf16[1024,128]{1,0:T(8,128)(2,1)S(1)}, u32[]{:S(2)}, u32[]{:S(2)}) collective-permute-start(bf16[1024,128]{1,0:T(8,128)(2,1)S(1)} %get-tuple-element.14), channel_id=1, source_target_pairs={{0,1},{1,0},{2,3},{3,2},{4,5},{5,4},{6,7},{7,6},{8,9},{9,8},{10,11... | collective-permute-start | bytes 786440 | tf_op jit(solution)/shard_map/ppermute | solution.py:264
  26.7 1.2 %collective-permute-done.2 = bf16[1024,128]{1,0:T(8,128)(2,1)S(1)} collective-permute-done((bf16[1024,128]{1,0:T(8,128)(2,1)S(1)}, bf16[1024,128]{1,0:T(8,128)(2,1)S(1)}, u32[]{:S(2)}, u32[]{:S(2)}) %collective-permute-start.2) | collective-permute-done | bytes 262176 | tf_op jit(solution)/shard_map/ppermute | solution.py:264
  27.9 0.1 add_convert_fusion
  27.9 19.6 %all_to_all.15 = bf16[16,64,128]{2,1,0:T(8,128)(2,1)S(1)} all-to-all(bf16[16,64,128]{2,1,0:T(8,128)(2,1)S(1)} %bitcast.27), channel_id=1, replica_groups=mesh['y'=4,'zh'=4,'x'=4,'zl'=2,'core'=2] {'x','y'}, dimensions={0} | all-to-all | bytes 524288 | tf_op jit(solution)/shard_map/all_to_all | solution.py:241
  47.6 10.4 %all_to_all.16 = bf16[8,64,128]{2,1,0:T(8,128)(2,1)S(1)} all-to-all(bf16[8,64,128]{2,1,0:T(8,128)(2,1)S(1)} %broadcast_in_dim.7), channel_id=1, replica_groups=mesh['y'=4,'zh'=4,'x'=4,'zl'=2,'core'=2] {'zh','zl'}, dimensions={0} | all-to-all | bytes 262144 | tf_op jit(solution)/shard_map/all_to_all | solution.py:241
  58.1 10.8 %all_to_all.17 = bf16[16,64,128]{2,1,0:T(8,128)(2,1)S(1)} all-to-all(bf16[16,64,128]{2,1,0:T(8,128)(2,1)S(1)} %broadcast_in_dim.8), channel_id=1, replica_groups=mesh['y'=4,'zh'=4,'x'=4,'zl'=2,'core'=2] {'x','y'}, dimensions={0} | all-to-all | bytes 524288 | tf_op jit(solution)/shard_map/all_to_all | solution.py:241
  68.9 4.1 %collective-permute-start.3 = (bf16[1024,128]{1,0:T(8,128)(2,1)S(1)}, bf16[1024,128]{1,0:T(8,128)(2,1)S(1)}, u32[]{:S(2)}, u32[]{:S(2)}) collective-permute-start(bf16[1024,128]{1,0:T(8,128)(2,1)S(1)} %bitcast.26), channel_id=1, source_target_pairs={{0,1},{1,0},{2,3},{3,2},{4,5},{5,4},{6,7},{7,6},{8,9},{9,8},{10,11... | collective-permute-start | bytes 786440 | tf_op jit(solution)/shard_map/ppermute | solution.py:270
  73.0 2.2 %copy.21 = bf16[128,32,128]{0,1,2:T(8,128)(2,1)} copy(bf16[128,32,128]{2,1,0:T(8,128)(2,1)S(1)} %bitcast.21) | data formatting | bytes 2097152 | tf_op jit(solution)/shard_map/reshape | solution.py:265
  75.2 0.0 collective-permute-done.3
  75.2 0.1 broadcast_select_fusion.1
  75.3 0.8 %maximum_convert_fusion = f32[800,128]{1,0:T(8,128)} fusion(bf16[1024,128]{1,0:T(8,128)(2,1)S(1)} %get-tuple-element.18, bf16[1024,128]{1,0:T(8,128)(2,1)S(1)} %get-tuple-element.17), kind=kLoop, calls=%fused_computation.5 | loop fusion | flops 409600 | bytes 933888 | tf_op jit(solution)/shard_map/slice | solution.py:275
  76.1 0.9 %fusion = f32[1152,128]{1,0:T(8,128)} fusion(bf16[1024,128]{1,0:T(8,128)(2,1)S(1)} %get-tuple-element.18, bf16[1024,128]{1,0:T(8,128)(2,1)S(1)} %get-tuple-element.17), kind=kLoop, calls=%fused_computation.2 | loop fusion | flops 589824 | bytes 1114112 | tf_op jit(solution)/shard_map/convert_element_type | solution.py:273
  (5 shorter events, 0.1 us)
Async XLA Ops:
  2.9 10.7 %collective-permute-start.1 = (bf16[4,32,128]{2,1,0:T(8,128)(2,1)S(1)}, bf16[4,32,128]{2,1,0:T(8,128)(2,1)S(1)}, u32[]{:S(2)}, u32[]{:S(2)}) collective-permute-start(bf16[4,32,128]{2,1,0:T(8,128)(2,1)S(1)} %get-tuple-element.15), channel_id=1, source_target_pairs={{16,0},{32,16},{48,32},{64,48},{80,64},{96,80},{112,96},{128,112},... | collective-permute-start | bytes 98312 | tf_op jit(solution)/shard_map/ppermute | solution.py:259
  4.2 9.4 %collective-permute-start = (bf16[4,32,128]{2,1,0:T(8,128)(2,1)S(1)}, bf16[4,32,128]{2,1,0:T(8,128)(2,1)S(1)}, u32[]{:S(2)}, u32[]{:S(2)}) collective-permute-start(bf16[4,32,128]{2,1,0:T(8,128)(2,1)S(1)} %get-tuple-element.16), channel_id=1, source_target_pairs={{0,16},{16,32},{32,48},{48,64},{64,80},{80,96},{96,112},{112,128},... | collective-permute-start | bytes 98312 | tf_op jit(solution)/shard_map/ppermute | solution.py:258
  10.6 2.5 %copy-start = (bf16[3,3,128,128]{3,2,1,0:T(8,128)(2,1)S(1)}, bf16[3,3,128,128]{3,2,1,0:T(8,128)(2,1)}, u32[]{:S(2)}) copy-start(bf16[3,3,128,128]{3,2,1,0:T(8,128)(2,1)} %k2.1) | copy-start | bytes 884740
  10.6 2.5 %copy-start.1 = (bf16[5,5,32,128]{3,2,1,0:T(8,128)(2,1)S(1)}, bf16[5,5,32,128]{3,2,1,0:T(8,128)(2,1)}, u32[]{:S(2)}) copy-start(bf16[5,5,32,128]{3,2,1,0:T(8,128)(2,1)} %k1.1) | copy-start | bytes 614404
  24.3 3.6 %collective-permute-start.2 = (bf16[1024,128]{1,0:T(8,128)(2,1)S(1)}, bf16[1024,128]{1,0:T(8,128)(2,1)S(1)}, u32[]{:S(2)}, u32[]{:S(2)}) collective-permute-start(bf16[1024,128]{1,0:T(8,128)(2,1)S(1)} %get-tuple-element.14), channel_id=1, source_target_pairs={{0,1},{1,0},{2,3},{3,2},{4,5},{5,4},{6,7},{7,6},{8,9},{9,8},{10,11... | collective-permute-start | bytes 786440 | tf_op jit(solution)/shard_map/ppermute | solution.py:264
  68.9 6.3 %collective-permute-start.3 = (bf16[1024,128]{1,0:T(8,128)(2,1)S(1)}, bf16[1024,128]{1,0:T(8,128)(2,1)S(1)}, u32[]{:S(2)}, u32[]{:S(2)}) collective-permute-start(bf16[1024,128]{1,0:T(8,128)(2,1)S(1)} %bitcast.26), channel_id=1, source_target_pairs={{0,1},{1,0},{2,3},{3,2},{4,5},{5,4},{6,7},{7,6},{8,9},{9,8},{10,11... | collective-permute-start | bytes 786440 | tf_op jit(solution)/shard_map/ppermute | solution.py:270

commit v5 on v4

--- a/solution.py
+++ b/solution.py
@@ -190,8 +190,51 @@
     total[1952:2048] = jnp.zeros((96, 128), F32)
     mine = pl.multiple_of(place[2] * 1024, 1024)
     other = pl.multiple_of((1 - place[2]) * 1024, 1024)
-    keep[...] = total[pl.ds(mine, 1024)]
+    keep[...] = total[pl.ds(mine, 1024)].astype(BF)
     send[...] = total[pl.ds(other, 1024)].astype(BF)
+
+
+def half_kernel(core, half, *refs):
+    grad_two, grad_one, wide, left = refs[-4:]
+    wide[...] = half[...].astype(F32)
+
+    @pl.when(core[0] == 0)
+    def _():
+        copy = pltpu.make_async_copy(wide, grad_two.at[pl.ds(0, 1024)], left.at[0])
+        copy.start()
+        copy.wait()
+
+    @pl.when(core[0] != 0)
+    def _():
+        two = pltpu.make_async_copy(
+            wide.at[pl.ds(0, 128)], grad_two.at[pl.ds(1024, 128)], left.at[0]
+        )
+        one = pltpu.make_async_copy(wide.at[pl.ds(128, 800)], grad_one, left.at[1])
+        two.start()
+        one.start()
+        two.wait()
+        one.wait()
+
+
+def write_half(core, half, *grads):
+    anywhere = pl.BlockSpec(memory_space=pl.ANY)
+    return pl.pallas_call(
+        half_kernel,
+        out_shape=(
+            jax.ShapeDtypeStruct((1152, 128), F32),
+            jax.ShapeDtypeStruct((800, 128), F32),
+        ),
+        in_specs=[
+            pl.BlockSpec(memory_space=pltpu.SMEM),
+            pl.BlockSpec(memory_space=pltpu.VMEM),
+        ]
+        + [anywhere] * len(grads),
+        out_specs=(anywhere, anywhere),
+        scratch_shapes=[pltpu.VMEM((1024, 128), F32), pltpu.SemaphoreType.DMA((2,))],
+        input_output_aliases={2: 0, 3: 1} if grads else {},
+        compiler_params=pltpu.CompilerParams(vmem_limit_bytes=8 * 1024 * 1024),
+        cost_estimate=pl.CostEstimate(flops=0, bytes_accessed=1_500_000, transcendentals=0),
+    )(core, half, *grads)
 
 
 def block(place, low, middle, high, w1, w2, wb, cot):
@@ -200,7 +243,7 @@
         block_kernel,
         out_shape=(
             jax.ShapeDtypeStruct((32, 2, 64, 128), BF),
-            jax.ShapeDtypeStruct((1024, 128), F32),
+            jax.ShapeDtypeStruct((1024, 128), BF),
             jax.ShapeDtypeStruct((1024, 128), BF),
         ),
         in_specs=[pl.BlockSpec(memory_space=pltpu.SMEM)] + [vmem] * 7,
@@ -263,17 +306,15 @@
     swap = [(0, 1), (1, 0)]
     sibling = lax.ppermute(send, "core", swap)
     feature_map = jnp.transpose(fmap.reshape(128, 32, 128), (2, 1, 0))[None]
-    chip_sum = (keep + sibling.astype(F32)).astype(BF)
+    sibling, feature_map = lax.optimization_barrier((sibling, feature_map))
+    chip_sum = (keep.astype(F32) + sibling.astype(F32)).astype(BF)
     layer_sum = summed(exchange(chip_sum.reshape(16, 64, 128), ("x", "y")))
     full_sum = summed(gathered(layer_sum, ("zh", "zl"), 8))
     half = gathered(full_sum, ("x", "y"), 16).reshape(1024, 128)
     rest = lax.ppermute(half, "core", swap)
-    rows = jnp.concatenate(
-        [jnp.where(core == 0, half, rest), jnp.where(core == 0, rest, half)], axis=0
-    ).astype(F32)
-    grad_two = rows[:1152].reshape(3, 3, 128, 128)
-    grad_one = rows[1152:1952].reshape(5, 5, 32, 128)
-    return (feature_map, grad_one, grad_two)
+    grads = write_half(core[None], half)
+    grad_two, grad_one = write_half(1 - core[None], rest, *grads)
+    return (feature_map, grad_one.reshape(5, 5, 32, 128), grad_two.reshape(3, 3, 128, 128))
 
 
 def solution(mesh):

time: 77.2 us -> 76.8 us (level)
  Pallas kernels: 11.1 us -> 13.5 us
  waiting for transfers between devices: 1.17 us -> 3.43 us
  blocking collectives: 40.8 us -> 39 us
  other arithmetic: 1.89 us -> 0.22 us
  starting transfers between devices: 14.1 us -> 12.6 us
    ppermute x1, waiting for transfers between devices: 0.01 us -> 3.09 us  [on_device(): high = lax.ppermute(middle[:4], TRACK, down)]
    all_to_all x3, blocking collectives: 40.8 us -> 39 us  [exchange(): return lax.all_to_all(pieces, axes, 0, 0, tiled=True)]
    pallas_call x0 -> x2, Pallas kernels: none -> 1.67 us  [write_half(): pl.pallas_call(half_kernel, out_shape=(jax.ShapeDtypeStruct((1152, 128),...]
    ppermute x1, waiting for transfers between devices: 1.16 us -> 0.01 us  [on_device(): sibling = lax.ppermute(send, 'core', swap)]
    convert_element_type x2 -> x1, other arithmetic: 0.91 us -> 0.07 us  [on_device(): chip_sum = (keep.astype(F32) + sibling.astype(F32)).astype(BF)]
    slice x1 -> x0, other arithmetic: 0.78 us -> none  [on_device(): grad_one = rows[1152:1952].reshape(5, 5, 32, 128)]
  transfers between devices with their start and end apart: 4 -> 4, of which waited for: 1 -> 2; matrix products, arithmetic and copies ran while one was open for 6% -> 6% of each run, Pallas kernels for 0% -> 2%
where the time goes in v5:
time: 76.8 us; the launch traced here: 76.5 us
  blocking collectives  39 us (51%)
  Pallas kernels  13.5 us (18%)
  starting transfers between devices  12.6 us (16%)
  local copies, waits for them, and re-layouts  7.04 us (9%)
  waiting for transfers between devices  3.43 us (4%)
    all_to_all x3, blocking collectives, exchange(): return lax.all_to_all(pieces, axes, 0, 0, tiled=True)  39 us
    pallas_call x1, Pallas kernels, block(): pl.pallas_call(block_kernel, out_shape=(jax.ShapeDtypeStruct((32, 2, 64,...  11.4 us
    ppermute x1, starting transfers between devices, on_device(): low = lax.ppermute(middle[124:], TRACK, up)  5.73 us
    ppermute x1, starting transfers between devices, on_device(): rest = lax.ppermute(half, 'core', swap)  3.79 us
    transpose x2, local copies, waits for them, and re-layouts, columns_first(): return jnp.transpose(block_of[0], (2, 1, 0))  3.58 us
    ppermute x1, waiting for transfers between devices, on_device(): high = lax.ppermute(middle[:4], TRACK, down)  3.09 us
    reshape x1, local copies, waits for them, and re-layouts, on_device(): feature_map = jnp.transpose(fmap.reshape(128, 32, 128), (2, 1, 0))[None]  2.24 us
    ppermute x1, starting transfers between devices, on_device(): sibling = lax.ppermute(send, 'core', swap)  1.83 us
  transfers between devices with their start and end apart: 4, of which 2 were waited for; matrix products, arithmetic and copies ran while one was open for 6% of the time, Pallas kernels for 2%

profile of v5, /device:TPU:1, one launch (start us, length us, event | category | flops | bytes accessed | tf_op | source)
XLA Modules:
  0.0 76.5 jit_solution(3300406296965090900)
XLA Ops:
  0.6 1.1 %copy.18 = bf16[128,32,32]{0,2,1:T(8,128)(2,1)S(1)} copy(bf16[128,32,32]{0,1,2:T(8,128)(2,1)} %bitcast.29) | data formatting | bytes 524288 | tf_op jit(solution)/shard_map/transpose | solution.py:272
  1.7 0.2 tile.4
  1.9 1.0 %copy.19.middle = bf16[128,32,128]{2,1,0:T(8,128)(2,1)S(1)} copy(bf16[128,32,128]{0,2,1:T(8,128)(2,1)S(1)} %bitcast.23) | data formatting | bytes 2097152 | tf_op jit(solution)/shard_map/optimization_barrier | solution.py:300
  2.9 5.7 %collective-permute-start = (bf16[4,32,128]{2,1,0:T(8,128)(2,1)S(1)}, bf16[4,32,128]{2,1,0:T(8,128)(2,1)S(1)}, u32[]{:S(2)}, u32[]{:S(2)}) collective-permute-start(bf16[4,32,128]{2,1,0:T(8,128)(2,1)S(1)} %get-tuple-element.28), channel_id=1, source_target_pairs={{0,16},{16,32},{32,48},{48,64},{64,80},{80,96},{96,112},{112,128},... | collective-permute-start | bytes 98312 | tf_op jit(solution)/shard_map/ppermute | solution.py:301
  8.6 1.3 %collective-permute-start.1 = (bf16[4,32,128]{2,1,0:T(8,128)(2,1)S(1)}, bf16[4,32,128]{2,1,0:T(8,128)(2,1)S(1)}, u32[]{:S(2)}, u32[]{:S(2)}) collective-permute-start(bf16[4,32,128]{2,1,0:T(8,128)(2,1)S(1)} %get-tuple-element.27), channel_id=1, source_target_pairs={{16,0},{32,16},{48,32},{64,48},{80,64},{96,80},{112,96},{128,112},... | collective-permute-start | bytes 98312 | tf_op jit(solution)/shard_map/ppermute | solution.py:302
  9.9 0.1 pad_add_fusion.place
  10.0 0.0 copy-start
  10.0 0.0 copy-start.1
  10.0 2.5 %copy.21 = bf16[128,32,128]{2,1,0:T(8,128)(2,1)S(1)} copy(bf16[128,32,128]{0,1,2:T(8,128)(2,1)} %bitcast.25) | data formatting | bytes 2097152 | tf_op jit(solution)/shard_map/transpose | solution.py:272
  12.5 0.0 copy-done
  12.5 0.0 copy-done.1
  12.5 0.4 shard_map.67
  12.9 0.0 collective-permute-done.low
  12.9 3.1 %collective-permute-done.1.high = bf16[4,32,128]{2,1,0:T(8,128)(2,1)S(1)} collective-permute-done((bf16[4,32,128]{2,1,0:T(8,128)(2,1)S(1)}, bf16[4,32,128]{2,1,0:T(8,128)(2,1)S(1)}, u32[]{:S(2)}, u32[]{:S(2)}) %collective-permute-start.1) | collective-permute-done | bytes 32800 | tf_op jit(solution)/shard_map/ppermute | solution.py:302
  16.0 11.4 %shard_map.68 = (bf16[32,2,64,128]{3,2,1,0:T(8,128)(2,1)S(1)}, bf16[1024,128]{1,0:T(8,128)(2,1)S(1)}, bf16[1024,128]{1,0:T(8,128)(2,1)}) custom-call(s32[3]{0:T(128)S(1)} %pad_add_fusion.place, bf16[4,32,128]{2,1,0:T(8,128)(2,1)S(1)} %collective-permute-done.low, bf16[128,32,128]{2,1,0:T(8,128)(2,1)S(1)} %copy.19.middle, ...), custom_call_target="tpu_custom_call" | custom-call | flops 5500000256 | bytes 5000000 | tf_op jit(solution)/shard_map/pallas_call | solution.py:242
  27.4 1.8 %collective-permute-start.2 = (bf16[1024,128]{1,0:T(8,128)(2,1)}, bf16[1024,128]{1,0:T(8,128)(2,1)S(1)}, u32[]{:S(2)}, u32[]{:S(2)}) collective-permute-start(bf16[1024,128]{1,0:T(8,128)(2,1)} %get-tuple-element.18), channel_id=1, source_target_pairs={{0,1},{1,0},{2,3},{3,2},{4,5},{5,4},{6,7},{7,6},{8,9},{9,8},{10,11... | collective-permute-start | bytes 786440 | tf_op jit(solution)/shard_map/ppermute | solution.py:307
  29.3 2.2 %copy.23 = bf16[128,32,128]{0,1,2:T(8,128)(2,1)} copy(bf16[128,32,128]{2,1,0:T(8,128)(2,1)S(1)} %bitcast.20) | data formatting | bytes 2097152 | tf_op jit(solution)/shard_map/reshape | solution.py:308
  31.5 0.0 collective-permute-done.2
  31.5 0.1 add_convert_fusion
  31.6 14.4 %all_to_all.15 = bf16[16,64,128]{2,1,0:T(8,128)(2,1)S(1)} all-to-all(bf16[16,64,128]{2,1,0:T(8,128)(2,1)S(1)} %bitcast.24), channel_id=1, replica_groups=mesh['y'=4,'zh'=4,'x'=4,'zl'=2,'core'=2] {'x','y'}, dimensions={0} | all-to-all | bytes 524288 | tf_op jit(solution)/shard_map/all_to_all | solution.py:284
  46.0 13.5 %all_to_all.16 = bf16[8,64,128]{2,1,0:T(8,128)(2,1)S(1)} all-to-all(bf16[8,64,128]{2,1,0:T(8,128)(2,1)S(1)} %broadcast_in_dim.7), channel_id=1, replica_groups=mesh['y'=4,'zh'=4,'x'=4,'zl'=2,'core'=2] {'zh','zl'}, dimensions={0} | all-to-all | bytes 262144 | tf_op jit(solution)/shard_map/all_to_all | solution.py:284
  59.6 11.1 %all_to_all.17 = bf16[16,64,128]{2,1,0:T(8,128)(2,1)S(1)} all-to-all(bf16[16,64,128]{2,1,0:T(8,128)(2,1)S(1)} %broadcast_in_dim.8), channel_id=1, replica_groups=mesh['y'=4,'zh'=4,'x'=4,'zl'=2,'core'=2] {'x','y'}, dimensions={0} | all-to-all | bytes 524288 | tf_op jit(solution)/shard_map/all_to_all | solution.py:284
  70.7 3.8 %collective-permute-start.3 = (bf16[1024,128]{1,0:T(8,128)(2,1)S(1)}, bf16[1024,128]{1,0:T(8,128)(2,1)S(1)}, u32[]{:S(2)}, u32[]{:S(2)}) collective-permute-start(bf16[1024,128]{1,0:T(8,128)(2,1)S(1)} %bitcast.21), channel_id=1, source_target_pairs={{0,1},{1,0},{2,3},{3,2},{4,5},{5,4},{6,7},{7,6},{8,9},{9,8},{10,11... | collective-permute-start | bytes 786440 | tf_op jit(solution)/shard_map/ppermute | solution.py:314
  74.5 0.8 %shard_map.69 = (f32[1152,128]{1,0:T(8,128)}, f32[800,128]{1,0:T(8,128)}) custom-call(s32[1]{0:T(128)} %bitcast.2.core, bf16[1024,128]{1,0:T(8,128)(2,1)S(1)} %bitcast.22), custom_call_target="tpu_custom_call" | custom-call | bytes 1500000 | tf_op jit(solution)/shard_map/pallas_call | solution.py:221
  75.4 0.3 collective-permute-done.3.half
  75.7 0.8 %shard_map.70 = (f32[1152,128]{1,0:T(8,128)}, f32[800,128]{1,0:T(8,128)}) custom-call(s32[1]{0:T(128)S(6)} %sub.3.core, bf16[1024,128]{1,0:T(8,128)(2,1)S(1)} %collective-permute-done.3.half, f32[1152,128]{1,0:T(8,128)} %get-tuple-element.23.refs_0_, f32[800,128]{1,0:T(8,128)} %get-tuple-element.24.refs_1_), custom_call_target="tpu_custom_call", output_to_operand_aliasing={{0}: (2, {}), {1}: (3, {})} | custom-call | bytes 1500000 | tf_op jit(solution)/shard_map/pallas_call | solution.py:221
  (5 shorter events, 0.1 us)
Async XLA Ops:
  2.9 10.0 %collective-permute-start = (bf16[4,32,128]{2,1,0:T(8,128)(2,1)S(1)}, bf16[4,32,128]{2,1,0:T(8,128)(2,1)S(1)}, u32[]{:S(2)}, u32[]{:S(2)}) collective-permute-start(bf16[4,32,128]{2,1,0:T(8,128)(2,1)S(1)} %get-tuple-element.28), channel_id=1, source_target_pairs={{0,16},{16,32},{32,48},{48,64},{64,80},{80,96},{96,112},{112,128},... | collective-permute-start | bytes 98312 | tf_op jit(solution)/shard_map/ppermute | solution.py:301
  8.6 7.4 %collective-permute-start.1 = (bf16[4,32,128]{2,1,0:T(8,128)(2,1)S(1)}, bf16[4,32,128]{2,1,0:T(8,128)(2,1)S(1)}, u32[]{:S(2)}, u32[]{:S(2)}) collective-permute-start(bf16[4,32,128]{2,1,0:T(8,128)(2,1)S(1)} %get-tuple-element.27), channel_id=1, source_target_pairs={{16,0},{32,16},{48,32},{64,48},{80,64},{96,80},{112,96},{128,112},... | collective-permute-start | bytes 98312 | tf_op jit(solution)/shard_map/ppermute | solution.py:302
  10.0 2.5 %copy-start = (bf16[3,3,128,128]{3,2,1,0:T(8,128)(2,1)S(1)}, bf16[3,3,128,128]{3,2,1,0:T(8,128)(2,1)}, u32[]{:S(2)}) copy-start(bf16[3,3,128,128]{3,2,1,0:T(8,128)(2,1)} %k2.1) | copy-start | bytes 884740
  10.0 2.5 %copy-start.1 = (bf16[5,5,32,128]{3,2,1,0:T(8,128)(2,1)S(1)}, bf16[5,5,32,128]{3,2,1,0:T(8,128)(2,1)}, u32[]{:S(2)}) copy-start(bf16[5,5,32,128]{3,2,1,0:T(8,128)(2,1)} %k1.1) | copy-start | bytes 614404
  27.4 4.1 %collective-permute-start.2 = (bf16[1024,128]{1,0:T(8,128)(2,1)}, bf16[1024,128]{1,0:T(8,128)(2,1)S(1)}, u32[]{:S(2)}, u32[]{:S(2)}) collective-permute-start(bf16[1024,128]{1,0:T(8,128)(2,1)} %get-tuple-element.18), channel_id=1, source_target_pairs={{0,1},{1,0},{2,3},{3,2},{4,5},{5,4},{6,7},{7,6},{8,9},{9,8},{10,11... | collective-permute-start | bytes 786440 | tf_op jit(solution)/shard_map/ppermute | solution.py:307
  70.7 5.0 %collective-permute-start.3 = (bf16[1024,128]{1,0:T(8,128)(2,1)S(1)}, bf16[1024,128]{1,0:T(8,128)(2,1)S(1)}, u32[]{:S(2)}, u32[]{:S(2)}) collective-permute-start(bf16[1024,128]{1,0:T(8,128)(2,1)S(1)} %bitcast.21), channel_id=1, source_target_pairs={{0,1},{1,0},{2,3},{3,2},{4,5},{5,4},{6,7},{7,6},{8,9},{9,8},{10,11... | collective-permute-start | bytes 786440 | tf_op jit(solution)/shard_map/ppermute | solution.py:314
